TPU v7x, 256 devices: a whole 4x4x8 slice. The times are simulated.
256 devices in a mesh: group: 8 (over x, core), dev: 32 (over z, y).
Axes of the slice: x: 4, y: 4, z: 8, core: 2. Of those that a mesh axis runs over, the one named last changes fastest.
Arguments:
- charges: float32 [64, 1048576], P(None, ('group', 'dev')), may hold values from -6 to 6
- coords: float32 [3, 1048576], P(None, ('group', 'dev')), may hold values from 0 to 1
- point_order: int32 [256, 4096], P(('group', 'dev')), may hold values from 0 to 4095, each once within a row
- near_list: int32 [8192, 27], P(('group', 'dev')), may hold values from 0 to 47
- send_list: int32 [256, 256], P(('group', 'dev')), may hold values from 0 to 31
- recv_list: int32 [256, 256], P(('group', 'dev')), may hold values from 0 to 255, each once within a row
- leaf_basis: float32 [32, 1048576], P(None, ('group', 'dev')), may hold values from -0.5 to 0.5
- local_transfer: float32 [15872, 1024], P(('group', 'dev')), may hold values from -0.75 to 0.75
- leaf_coupling: float32 [65536, 1024], P(('group', 'dev')), may hold values from -0.375 to 0.375
- group_transfer: float32 [496, 1024], P('group'), may hold values from -0.75 to 0.75
- top_coupling: float32 [8, 32, 256], P('group'), may hold values from -0.375 to 0.375
Outputs:
- potential: float32 [64, 1048576], P(None, ('group', 'dev'))
Inputs may be any that keep to these rules, and one draw needn't show every extreme that they name: `point_order`: each row is a permutation of 0 to 4095. `recv_list`: each row is a permutation of 0 to 255.
All inputs are finite; a program needn't handle non-finite values.
Results may differ from a plain program's by a relative error of at most 0.0003.
Values sent between devices are 32-bit elements; how exact they have to be, the bound alone decides.
No kernel may reach another device: no remote copies, remote signals or barrier semaphores. Data moves between devices by JAX's collectives and lax.ppermute only.
A program may use at most 64 MiB of HBM per device.

v0:
```python
import functools

import jax
import jax.numpy as jnp
from jax import lax
from jax.experimental import pallas as pl
from jax.experimental.pallas import tpu as pltpu
from jax.sharding import PartitionSpec as P

f32 = jnp.float32
bf16 = jnp.bfloat16
highest = lax.Precision.HIGHEST

LEAF = 128
RANK = 32
RHS = 64
LEAVES = 32
PTS = 4096
NEAR = 27
CHUNK = 14
HALO_L = 8
HALO = HALO_L * LEAF
WIN_L = LEAVES + 2 * HALO_L
WIN = WIN_L * LEAF
INTER = 8
GROUPS = 8
MEMBERS = 32
PACK = HALO // 2 + 8 * HALO_L
FEATURES = 48

LOG2E = 1.4426950408889634
SCALE = LOG2E * 3.0**0.5 / 0.3
FLOOR = SCALE * SCALE * 1e-6
WEIGHT = 0.1 / LOG2E
DOWN = 2.0**0.5
VMEM_BYTES = 48 * 1024 * 1024

vmem = pl.BlockSpec(memory_space=pltpu.VMEM)
smem = pl.BlockSpec(memory_space=pltpu.SMEM)


def block(index, size):
    return pl.ds(pl.multiple_of(index * size, size), size)


def dot(a, b):
    return jnp.dot(a, b, precision=highest, preferred_element_type=f32)


def left_half(shape):
    return lax.broadcasted_iota(jnp.int32, shape, len(shape) - 1) < RHS


def swap(x):
    return pltpu.roll(x, RHS, 1)


def both(x):
    return jnp.where(left_half(x.shape), x, swap(x))


def fold(x):
    half = RANK // 2
    return jnp.where(left_half((half, 2 * RHS)), x[:half], swap(x[half:]))


def unfold(x):
    return jnp.concatenate([x, swap(x)], axis=0)


def two(x):
    high = x.astype(bf16)
    return high, (x - high.astype(f32)).astype(bf16)


def three(x):
    high = x.astype(bf16).astype(f32)
    rest = x - high
    middle = rest.astype(bf16).astype(f32)
    return high, middle, rest - middle


def order_kernel(
    order_ref, send_ref, charges_ref, coords_ref, basis_ref,
    rows_ref, places_ref, first_ref, last_ref, coef_ref, sent_ref,
    turned_ref, padded_ref,
):
    padded_ref[...] = jnp.zeros_like(padded_ref)
    padded_ref[0:3, :] = coords_ref[...]

    def turn(b, carry):
        columns = block(b, LEAF)
        tall = jnp.concatenate(
            [charges_ref[:, columns], padded_ref[:, columns], jnp.zeros((56, LEAF), f32)], axis=0
        )
        turned_ref[columns, :] = tall.T
        return carry

    lax.fori_loop(0, LEAVES, turn, 0)

    def fetch(b, carry):
        for i in range(32):
            at = b * 32 + i
            rows_ref[pl.ds(at, 1), :] = turned_ref[pl.ds(order_ref[0, at], 1), :]
        return carry

    lax.fori_loop(0, PTS // 32, fetch, 0)

    def coefficient(l, carry):
        columns = block(l, LEAF)
        rows = rows_ref[columns, :]
        coef_ref[l] = both(dot(basis_ref[:, columns], rows))
        places_ref[:, columns] = rows.T[RHS : RHS + 8]
        return carry

    lax.fori_loop(0, LEAVES, coefficient, 0)

    for ref, start in ((first_ref, 0), (last_ref, PTS - HALO)):
        near = rows_ref[start : start + HALO // 2, :]
        far = rows_ref[start + HALO // 2 : start + HALO, :]
        ref[: HALO // 2, :] = jnp.where(left_half(near.shape), near, swap(far))
        for i in range(HALO_L):
            ref[HALO // 2 + 8 * i : HALO // 2 + 8 * i + 8, :] = places_ref[
                :, start + i * LEAF : start + (i + 1) * LEAF
            ]

    left = left_half((RANK, 2 * RHS))

    def pack(d, carry):
        for q in range(4):
            one = coef_ref[send_ref[0, d * 8 + 2 * q]]
            other = coef_ref[send_ref[0, d * 8 + 2 * q + 1]]
            sent_ref[d, q * RANK : (q + 1) * RANK, :] = jnp.where(left, one, other)
        return carry

    lax.fori_loop(0, MEMBERS, pack, 0)


def near_kernel(
    list_ref, bias_ref, rows_ref, places_ref, before_ref, after_ref,
    out_ref, target_ref, source_ref, weight_ref,
):
    row = lax.broadcasted_iota(jnp.int32, (8, LEAF), 0)
    zero = jnp.zeros((8, LEAF), f32)

    def features(w, places):
        c = jnp.where(row < 3, (places - 0.5) * SCALE, 0.0)
        squares = jnp.sum(c * c, axis=0, keepdims=True) + 0.5 * FLOOR
        parts = three(jnp.broadcast_to(squares, (8, LEAF)))
        h, m, l = three(c)
        norm = jnp.where(row == 3, parts[0], jnp.where(row == 4, parts[1], parts[2]))
        is_norm = jnp.logical_and(row >= 3, row < 6)
        norm = jnp.where(is_norm, norm, 0.0)
        ones = jnp.where(is_norm, 1.0, 0.0)
        columns = block(w, LEAF)
        source = jnp.concatenate([h + ones, m + norm, l, h, m, h], axis=0)
        source_ref[:, columns] = source.astype(bf16)
        target = jnp.concatenate(
            [-2.0 * h + norm, -2.0 * h + ones, -2.0 * h, -2.0 * m, -2.0 * m, -2.0 * l], axis=0
        )
        return target

    def weigh(w, x):
        scaled = x * WEIGHT
        high = scaled.astype(bf16).astype(f32)
        low = scaled - high
        both_parts = jnp.where(left_half(x.shape), high, swap(low))
        weight_ref[block(w, LEAF), :] = both_parts.astype(bf16)

    def own(b, carry):
        columns = block(b, LEAF)
        target = features(b + HALO_L, places_ref[:, columns])
        target = jnp.concatenate([target] + [zero] * 10, axis=0)
        target_ref[columns, :] = target.T[:, :FEATURES].astype(bf16)
        weigh(b + HALO_L, rows_ref[columns, :])
        return carry

    lax.fori_loop(0, LEAVES, own, 0)
    for ref, start in ((before_ref, 0), (after_ref, HALO_L + LEAVES)):
        for i in range(HALO_L):
            features(start + i, ref[HALO // 2 + 8 * i : HALO // 2 + 8 * i + 8, :])
            x = ref[(i % 4) * LEAF : (i % 4 + 1) * LEAF, :]
            weigh(start + i, x if i < 4 else swap(x))

    def leaf(a, carry):
        target = target_ref[block(a, LEAF), :]
        total = jnp.zeros((LEAF, 2 * RHS), f32)
        for j in range(0, NEAR + 1, CHUNK):
            at = [block(list_ref[a, j + i], LEAF) for i in range(CHUNK)]
            source = jnp.concatenate([source_ref[:, s] for s in at], axis=1)
            weight = jnp.concatenate([weight_ref[s, :] for s in at], axis=0)
            squared = jnp.dot(target, source, preferred_element_type=f32)
            parts = []
            for i in range(CHUNK):
                r = jnp.maximum(squared[:, i * LEAF : (i + 1) * LEAF], FLOOR)
                t = r * lax.rsqrt(r)
                parts.append((t + LOG2E) * jnp.exp2(bias_ref[a, j + i] - t))
            high, low = two(jnp.concatenate(parts, axis=1))
            first = jnp.dot(high, weight, preferred_element_type=f32)
            second = jnp.dot(low, weight, preferred_element_type=f32)
            total = total + (first + swap(first) + second)
        out_ref[:, block(a, LEAF)] = total.T[:RHS]
        return carry

    lax.fori_loop(0, LEAVES, leaf, 0)


def up_kernel(place_ref, coef_ref, pair_ref, path_ref, out_ref, level_ref):
    level_ref[...] = coef_ref[...].reshape(level_ref.shape)
    offset, count = 0, LEAVES
    while count > 1:
        values = [
            dot(pair_ref[offset + i], level_ref[2 * RANK * i : 2 * RANK * (i + 1), :])
            for i in range(count // 2)
        ]
        for i, value in enumerate(values):
            level_ref[RANK * i : RANK * (i + 1), :] = value
        offset, count = offset + count // 2, count // 2
    value = level_ref[:RANK, :]
    position = place_ref[0]
    offset, count = 0, MEMBERS
    while count > 1:
        value = dot(path_ref[offset + position], value)
        offset, count, position = offset + count, count // 2, lax.shift_right_logical(position, 1)
    packed = fold(value)
    for g in range(GROUPS):
        out_ref[g] = packed


def top_kernel(roots_ref, coupling_ref, out_ref):
    stacked = jnp.concatenate([unfold(roots_ref[g]) for g in range(GROUPS)], axis=0)
    packed = fold(dot(coupling_ref[0], stacked))
    for d in range(MEMBERS):
        out_ref[d] = packed


def final_kernel(
    place_ref, recv_ref, tops_ref, path_ref, pair_ref, slots_ref, coupling_ref, basis_ref, near_ref,
    out_ref, level_ref,
):
    folded = tops_ref[0]
    for d in range(1, MEMBERS):
        folded = folded + tops_ref[d]
    value = both(unfold(folded))
    position = place_ref[0]
    offset, count = 2 * MEMBERS - 4, 2
    while count <= MEMBERS:
        child = position // (MEMBERS // count)
        value = DOWN * dot(path_ref[offset + child], value)
        count = count * 2
        offset = offset - count
    nodes = [value]
    offset = LEAVES - 2
    while len(nodes) < LEAVES:
        children = [DOWN * dot(pair_ref[offset + i], node) for i, node in enumerate(nodes)]
        nodes = [c[RANK * k : RANK * (k + 1)] for c in children for k in (0, 1)]
        offset = offset - len(nodes)
    for i, node in enumerate(nodes):
        level_ref[i] = node

    left = left_half((RANK, 2 * RHS))

    def far(a):
        picked = []
        for j in range(INTER):
            slot = recv_ref[0, a * INTER + j]
            use_left = (slot & 1) == 0
            picked.append(
                jnp.where(left == use_left, slots_ref[lax.shift_right_logical(slot, 1)], 0.0)
            )
        y = dot(coupling_ref[a], jnp.concatenate(picked, axis=0))
        return y + swap(y) + level_ref[a]

    def finish(i, carry):
        joined = jnp.where(left, far(2 * i), far(2 * i + 1))
        joined = jnp.concatenate([joined, jnp.zeros((3 * RANK, 2 * RHS), f32)], axis=0).T[:, :RANK]
        columns = block(i, 2 * LEAF)
        y = dot(joined, basis_ref[:, columns])
        y = jnp.concatenate([y[:RHS, :LEAF], y[RHS:, LEAF:]], axis=1)
        out_ref[:, columns] = near_ref[:, columns] + y
        return carry

    lax.fori_loop(0, LEAVES // 2, finish, 0)


def call(kernel, name, outs, specs, scratch, flops):
    return pl.pallas_call(
        kernel,
        name=name,
        out_shape=[jax.ShapeDtypeStruct(s, f32) for s in outs],
        in_specs=specs,
        out_specs=[vmem] * len(outs),
        scratch_shapes=scratch,
        compiler_params=pltpu.CompilerParams(vmem_limit_bytes=VMEM_BYTES),
        cost_estimate=pl.CostEstimate(flops=flops, bytes_accessed=2**20, transcendentals=0),
    )


def shards(
    charges,
    coords,
    point_order,
    near_list,
    send_list,
    recv_list,
    leaf_basis,
    local_transfer,
    leaf_coupling,
    group_transfer,
    top_coupling,
):
    place = lax.axis_index("dev").astype(jnp.int32).reshape(1)
    rows, places, first, last, coef, sent = call(
        order_kernel,
        "order",
        [
            (PTS, LEAF), (8, PTS), (PACK, LEAF), (PACK, LEAF),
            (LEAVES, RANK, 2 * RHS), (MEMBERS, 4 * RANK, 2 * RHS),
        ],
        [smem, smem, vmem, vmem, vmem],
        [pltpu.VMEM((PTS, LEAF), f32), pltpu.VMEM((8, PTS), f32)],
        10**10,
    )(point_order, send_list, charges, coords, leaf_basis)
    size = lax.axis_size("group") * lax.axis_size("dev")
    up = [(i, i + 1) for i in range(size - 1)]
    down = [(i + 1, i) for i in range(size - 1)]
    before = lax.ppermute(last, ("group", "dev"), up)
    after = lax.ppermute(first, ("group", "dev"), down)
    slots = lax.all_to_all(sent, "dev", split_axis=0, concat_axis=0, tiled=True)

    local = local_transfer.reshape(LEAVES - 1, 2, RANK, RANK)
    up_pairs = jnp.swapaxes(local, 1, 2).reshape(LEAVES - 1, RANK, 2 * RANK)
    down_pairs = jnp.swapaxes(local, 2, 3).reshape(LEAVES - 1, 2 * RANK, RANK)
    group = group_transfer.reshape(2 * MEMBERS - 2, RANK, RANK)
    group_turned = jnp.swapaxes(group, 1, 2)
    (roots,) = call(
        up_kernel,
        "up",
        [(GROUPS, RANK // 2, 2 * RHS)],
        [smem, vmem, vmem, vmem],
        [pltpu.VMEM((LEAVES * RANK, 2 * RHS), f32)],
        5 * 10**9,
    )(place, coef, up_pairs, group)
    roots = lax.all_to_all(roots, "group", split_axis=0, concat_axis=0, tiled=True)
    (tops,) = call(
        top_kernel,
        "top",
        [(MEMBERS, RANK // 2, 2 * RHS)],
        [vmem, vmem],
        [],
        10**9,
    )(roots, top_coupling)
    tops = lax.all_to_all(tops, "dev", split_axis=0, concat_axis=0, tiled=True)

    listed = jnp.pad(near_list, ((0, 0), (0, 1)))
    bias = jnp.where(jnp.arange(NEAR + 1) < NEAR, 0.0, -1e4).astype(f32)
    bias = jnp.broadcast_to(bias, listed.shape)
    (near,) = call(
        near_kernel,
        "near",
        [(RHS, PTS)],
        [smem, smem, vmem, vmem, vmem, vmem],
        [
            pltpu.VMEM((PTS, FEATURES), bf16),
            pltpu.VMEM((FEATURES, WIN), bf16),
            pltpu.VMEM((WIN, 2 * RHS), bf16),
        ],
        5 * 10**10,
    )(listed, bias, rows, places, before, after)

    coupling = jnp.swapaxes(leaf_coupling.reshape(LEAVES, INTER, RANK, RANK), 1, 2)
    coupling = coupling.reshape(LEAVES, RANK, INTER * RANK)
    (potential,) = call(
        final_kernel,
        "final",
        [(RHS, PTS)],
        [smem, smem, vmem, vmem, vmem, vmem, vmem, vmem, vmem],
        [pltpu.VMEM((LEAVES, RANK, 2 * RHS), f32)],
        10**10,
    )(
        place, recv_list, tops, group_turned, down_pairs,
        slots.reshape(4 * MEMBERS, RANK, 2 * RHS), coupling, leaf_basis, near,
    )
    return potential


def solution(mesh):
    return jax.shard_map(
        shards,
        mesh=mesh,
        in_specs=(
            P(None, ("group", "dev")),
            P(None, ("group", "dev")),
            P(("group", "dev"), None),
            P(("group", "dev"), None),
            P(("group", "dev"), None),
            P(("group", "dev"), None),
            P(None, ("group", "dev")),
            P(("group", "dev"), None),
            P(("group", "dev"), None),
            P("group", None),
            P("group", None, None),
        ),
        out_specs=P(None, ("group", "dev")),
        check_vma=False,
    )
```

profile of v0, /device:TPU:17, one launch (start us, length us, event | category | flops | bytes accessed | tf_op | source)
XLA Modules:
  0.0 153.8 jit_solution(7132586448374265012)
XLA Ops:
  0.0 2.0 %copy.17 = f32[62,1024]{0,1:T(8,128)} copy(f32[62,1024]{1,0:T(8,128)} %param.20) | data formatting | bytes 507904 | tf_op args[9]
  2.0 1.3 reshape.25
  3.3 0.0 copy-start
  3.3 0.0 copy-start.1
  3.3 0.0 copy-start.3
  3.3 0.0 copy-start.5
  3.3 0.0 copy-start.6
  3.3 1.7 %copy.25 = f32[31,2,32,32]{3,1,2,0:T(2,128)} copy(f32[31,2,32,32]{3,2,1,0:T(8,128)S(1)} %reshape.25) | data formatting | bytes 507904 | tf_op jit(solution)/shard_map/reshape | solution.py:331
  5.1 1.8 %reshape.26.pair_ref = f32[31,32,64]{2,1,0:T(8,128)S(1)} reshape(f32[31,32,2,32]{3,2,1,0:T(2,128)} %bitcast.20) | data formatting | bytes 507904 | tf_op jit(solution)/shard_map/reshape | solution.py:332
  6.9 1.9 %copy.18.path_ref = f32[62,32,32]{2,1,0:T(8,128)S(1)} copy(f32[62,32,32]{0,2,1:T(8,128)} %bitcast.18) | data formatting | bytes 507904 | tf_op jit(solution)/shard_map/reshape | solution.py:334
  8.8 18.7 %order.1 = (f32[4096,128]{1,0:T(8,128)S(1)}, f32[8,4096]{1,0:T(8,128)S(1)}, f32[576,128]{1,0:T(8,128)}, f32[576,128]{1,0:T(8,128)}, f32[32,32,128]{2,1,0:T(8,128)S(1)}, /*index=5*/f32[32,128,128]{2,1,0:T(8,128)}) custom-call(s32[1,4096]{1,0:T(1,128)S(1)} %copy-done.5, s32[1,256]{1,0:T(1,128)S(1)} %copy-done.6, f32[64,4096]{1,0:T(8,128)S(1)} %copy-done, ...), custom_call_target="tpu_custom_call" | custom-call | flops 10000000000 | bytes 1048576 | tf_op jit(solution)/shard_map/order/pallas_call | solution.py:313
  27.6 1.3 copy-done.8
  28.9 2.0 %up.1 = f32[8,16,128]{2,1,0:T(8,128)S(1)} custom-call(s32[1]{0:T(128)} %bitcast.place_ref, f32[32,32,128]{2,1,0:T(8,128)S(1)} %get-tuple-element.11.coef_ref, f32[31,32,64]{2,1,0:T(8,128)S(1)} %reshape.26.pair_ref, f32[62,32,32]{2,1,0:T(8,128)S(1)} %copy.18.path_ref), custom_call_target="tpu_custom_call" | custom-call | flops 5000000000 | bytes 1048576 | tf_op jit(solution)/shard_map/up/pallas_call | solution.py:336
  30.9 9.7 %all_to_all.15.roots_ref = f32[8,16,128]{2,1,0:T(8,128)S(1)} all-to-all(f32[8,16,128]{2,1,0:T(8,128)S(1)} %up.1), channel_id=1, replica_groups=mesh['group'=8,'dev'=32] {'group'}, dimensions={0} | all-to-all | bytes 131072 | tf_op jit(solution)/shard_map/all_to_all | solution.py:344
  40.6 1.0 top.1
  41.6 11.2 %all-to-all-start.1 = ((f32[32,16,128]{2,1,0:T(8,128)}), f32[32,16,128]{2,1,0:T(8,128)S(1)}, u32[]{:S(2)}, u32[]{:S(2)}) async-start(f32[32,16,128]{2,1,0:T(8,128)} %top.1), calls=%async_computation.1 | async-start | bytes 524288 | tf_op jit(solution)/shard_map/all_to_all | solution.py:353
  52.8 2.8 %collective-permute-start = (f32[576,128]{1,0:T(8,128)}, f32[576,128]{1,0:T(8,128)}, u32[]{:S(2)}, u32[]{:S(2)}) collective-permute-start(f32[576,128]{1,0:T(8,128)} %get-tuple-element.15), channel_id=1, source_target_pairs={{0,1},{1,2},{2,3},{3,4},{4,5},{5,6},{6,7},{7,8},{8,9},{9,10},{10,1... | collective-permute-start | bytes 884744 | tf_op jit(solution)/shard_map/ppermute | solution.py:327
  55.6 2.5 %collective-permute-start.1 = (f32[576,128]{1,0:T(8,128)}, f32[576,128]{1,0:T(8,128)}, u32[]{:S(2)}, u32[]{:S(2)}) collective-permute-start(f32[576,128]{1,0:T(8,128)} %get-tuple-element.16), channel_id=1, source_target_pairs={{1,0},{2,1},{3,2},{4,3},{5,4},{6,5},{7,6},{8,7},{9,8},{10,9},{11,1... | collective-permute-start | bytes 884744 | tf_op jit(solution)/shard_map/ppermute | solution.py:328
  58.1 0.3 copy.20
  58.4 0.9 copy.19
  59.3 4.0 %reshape.30 = f32[32,8,32,32]{3,2,1,0:T(8,128)} reshape(f32[256,1024]{1,0:T(8,128)} %param.19) | data formatting | bytes 2097152 | tf_op jit(solution)/shard_map/reshape | solution.py:371
  63.3 8.0 %copy.24 = f32[32,8,32,32]{3,1,2,0:T(8,128)} copy(f32[32,8,32,32]{3,2,1,0:T(8,128)} %reshape.30) | data formatting | bytes 2097152 | tf_op jit(solution)/shard_map/reshape | solution.py:371
  71.3 3.4 %reshape.31.coupling_ref = f32[32,32,256]{2,1,0:T(8,128)S(1)} reshape(f32[32,32,8,32]{3,2,1,0:T(8,128)} %bitcast.17) | data formatting | bytes 2097152 | tf_op jit(solution)/shard_map/reshape | solution.py:372
  74.7 0.0 all-to-all-done.1.tops_ref
  74.7 10.2 %all-to-all-start.2 = ((f32[32,128,128]{2,1,0:T(8,128)}), f32[32,128,128]{2,1,0:T(8,128)}, u32[]{:S(2)}, u32[]{:S(2)}) async-start(f32[32,128,128]{2,1,0:T(8,128)} %get-tuple-element.12), calls=%async_computation.2 | async-start | bytes 4194304 | tf_op jit(solution)/shard_map/all_to_all | solution.py:329
  84.9 1.6 %copy-done.9 = f32[4096,128]{1,0:T(8,128)S(1)} copy-done((f32[4096,128]{1,0:T(8,128)S(1)}, f32[4096,128]{1,0:T(8,128)}, u32[]{:S(2)}) %copy-start.9) | copy-done | bytes 2097176
  86.5 49.1 %near.1.near_ref = f32[64,4096]{1,0:T(8,128)S(1)} custom-call(s32[32,28]{1,0:T(8,128)S(1)} %pad.4.list_ref, f32[32,28]{1,0:T(8,128)S(1)} %broadcast_in_dim.13.bias_ref, f32[4096,128]{1,0:T(8,128)S(1)} %copy-done.9, f32[8,4096]{1,0:T(8,128)S(1)} %get-tuple-element.14.places_ref, f32[576,128]{1,0:T(8,128)} %collective-permute-done.before_ref, ...), custom_call_target="tpu_custom_call" | custom-call | flops 49999998976 | bytes 1048576 | tf_op jit(solution)/shard_map/near/pallas_call | solution.py:358
  135.6 0.0 copy-start.10
  135.6 1.0 copy-done.10
  136.6 1.0 copy-done.2
  137.7 1.2 copy-done.11
  138.9 15.0 %final.1 = f32[64,4096]{1,0:T(8,128)} custom-call(s32[1]{0:T(128)} %bitcast.place_ref, s32[1,256]{1,0:T(1,128)S(1)} %copy-done.7, f32[32,16,128]{2,1,0:T(8,128)S(1)} %all-to-all-done.1.tops_ref, f32[62,32,32]{2,1,0:T(8,128)S(1)} %bitcast.15, f32[31,64,32]{2,1,0:T(8,128)S(1)} %bitcast.16, f32[128,32,128]{2,1,0:T(8,128)} %bitcast.6.slots_ref, ...), custom_call_target="tpu_custom_call" | custom-call | flops 10000000000 | bytes 1048576 | tf_op jit(solution)/shard_map/final/pallas_call | solution.py:373
  (27 shorter events, 0.1 us)
Async XLA Ops:
  3.3 3.6 %copy-start.12 = (f32[31,2,32,32]{3,2,1,0:T(8,128)}, f32[31,2,32,32]{3,2,1,0:T(8,128)S(1)}, u32[]{:S(2)}) copy-start(f32[31,2,32,32]{3,2,1,0:T(8,128)S(1)} %reshape.25) | copy-start | bytes 761860
  3.3 5.5 %copy-start = (f32[64,4096]{1,0:T(8,128)S(1)}, f32[64,4096]{1,0:T(8,128)}, u32[]{:S(2)}) copy-start(f32[64,4096]{1,0:T(8,128)} %charges_ref.1) | copy-start | bytes 3145732
  3.3 5.5 %copy-start.1 = (f32[32,4096]{1,0:T(8,128)S(1)}, f32[32,4096]{1,0:T(8,128)}, u32[]{:S(2)}) copy-start(f32[32,4096]{1,0:T(8,128)} %basis_ref.3) | copy-start | bytes 1572868
  3.3 5.5 %copy-start.3 = (f32[3,4096]{1,0:T(4,128)S(1)}, f32[3,4096]{1,0:T(4,128)}, u32[]{:S(2)}) copy-start(f32[3,4096]{1,0:T(4,128)} %coords_ref.1) | copy-start | bytes 147460
  3.3 5.5 %copy-start.5 = (s32[1,4096]{1,0:T(1,128)S(1)}, s32[1,4096]{1,0:T(1,128)}, u32[]{:S(2)}) copy-start(s32[1,4096]{1,0:T(1,128)} %order_ref.1) | copy-start | bytes 49156
  3.3 5.5 %copy-start.6 = (s32[1,256]{1,0:T(1,128)S(1)}, s32[1,256]{1,0:T(1,128)}, u32[]{:S(2)}) copy-start(s32[1,256]{1,0:T(1,128)} %send_ref.1) | copy-start | bytes 3076
  27.6 1.3 copy-start.8
  28.9 11.7 %copy-start.4 = (f32[1,32,256]{2,1,0:T(8,128)S(1)}, f32[1,32,256]{2,1,0:T(8,128)}, u32[]{:S(2)}) copy-start(f32[1,32,256]{2,1,0:T(8,128)} %coupling_ref.1) | copy-start | bytes 98308
  40.6 17.5 %copy-start.13 = (f32[31,2,32,32]{3,2,1,0:T(8,128)S(1)}, f32[31,2,32,32]{3,2,1,0:T(8,128)}, u32[]{:S(2)}) copy-start(f32[31,2,32,32]{3,2,1,0:T(8,128)} %copy-done.12) | copy-start | bytes 761860
  41.6 16.8 %copy-start.14 = (f32[62,1024]{0,1:T(8,128)S(1)}, f32[62,1024]{0,1:T(8,128)}, u32[]{:S(2)}) copy-start(f32[62,1024]{0,1:T(8,128)} %copy.17) | copy-start | bytes 761860
  41.6 33.1 %all-to-all-start.1 = ((f32[32,16,128]{2,1,0:T(8,128)}), f32[32,16,128]{2,1,0:T(8,128)S(1)}, u32[]{:S(2)}, u32[]{:S(2)}) async-start(f32[32,16,128]{2,1,0:T(8,128)} %top.1), calls=%async_computation.1 | async-start | bytes 524288 | tf_op jit(solution)/shard_map/all_to_all | solution.py:353
  52.8 32.1 %collective-permute-start = (f32[576,128]{1,0:T(8,128)}, f32[576,128]{1,0:T(8,128)}, u32[]{:S(2)}, u32[]{:S(2)}) collective-permute-start(f32[576,128]{1,0:T(8,128)} %get-tuple-element.15), channel_id=1, source_target_pairs={{0,1},{1,2},{2,3},{3,4},{4,5},{5,6},{6,7},{7,8},{8,9},{9,10},{10,1... | collective-permute-start | bytes 884744 | tf_op jit(solution)/shard_map/ppermute | solution.py:327
  55.6 29.3 %collective-permute-start.1 = (f32[576,128]{1,0:T(8,128)}, f32[576,128]{1,0:T(8,128)}, u32[]{:S(2)}, u32[]{:S(2)}) collective-permute-start(f32[576,128]{1,0:T(8,128)} %get-tuple-element.16), channel_id=1, source_target_pairs={{1,0},{2,1},{3,2},{4,3},{5,4},{6,5},{7,6},{8,7},{9,8},{10,9},{11,1... | collective-permute-start | bytes 884744 | tf_op jit(solution)/shard_map/ppermute | solution.py:328
  71.3 3.4 %copy-start.15 = (s32[32,27]{1,0:T(8,128)S(1)}, s32[32,27]{1,0:T(8,128)}, u32[]{:S(2)}) copy-start(s32[32,27]{1,0:T(8,128)} %param.14) | copy-start | bytes 10372
  74.7 61.9 %all-to-all-start.2 = ((f32[32,128,128]{2,1,0:T(8,128)}), f32[32,128,128]{2,1,0:T(8,128)}, u32[]{:S(2)}, u32[]{:S(2)}) async-start(f32[32,128,128]{2,1,0:T(8,128)} %get-tuple-element.12), calls=%async_computation.2 | async-start | bytes 4194304 | tf_op jit(solution)/shard_map/all_to_all | solution.py:329
  84.9 1.6 %copy-start.9 = (f32[4096,128]{1,0:T(8,128)S(1)}, f32[4096,128]{1,0:T(8,128)}, u32[]{:S(2)}) copy-start(f32[4096,128]{1,0:T(8,128)} %copy-done.8) | copy-start | bytes 6291460
  86.5 50.1 %copy-start.7 = (s32[1,256]{1,0:T(1,128)S(1)}, s32[1,256]{1,0:T(1,128)}, u32[]{:S(2)}) copy-start(s32[1,256]{1,0:T(1,128)} %recv_ref.1) | copy-start | bytes 3076
  135.6 1.0 copy-start.10
  136.6 1.0 copy-start.2
  137.7 1.2 copy-start.11
where the time goes:
time: 156 us; the launch traced here: 154 us
  Pallas kernels  85.8 us (55%)
  local copies, waits for them, and re-layouts  31.4 us (20%)
  starting transfers between devices  26.6 us (17%)
  blocking collectives  9.7 us (6%)
    pallas_call x1, Pallas kernels, shards(): call(near_kernel, 'near', [(RHS, PTS)], [smem, smem, vmem, vmem, vmem, vm...  49.1 us
    pallas_call x1, Pallas kernels, shards(): call(order_kernel, 'order', [(PTS, LEAF), (8, PTS), (PACK, LEAF), (PACK,...  18.7 us
    pallas_call x1, Pallas kernels, shards(): call(final_kernel, 'final', [(RHS, PTS)], [smem, smem, vmem, vmem, vmem,...  15 us
    reshape x2, local copies, waits for them, and re-layouts, shards(): leaf_coupling.reshape(LEAVES, INTER, RANK, RANK)  11.9 us
    all_to_all x1, starting transfers between devices, shards(): tops = lax.all_to_all(tops, 'dev', split_axis=0, concat_axis=0, tiled=True)  11.2 us
    all_to_all x1, starting transfers between devices, shards(): slots = lax.all_to_all(sent, 'dev', split_axis=0, concat_axis=0, tiled=True)  10.2 us
    all_to_all x1, blocking collectives, shards(): lax.all_to_all(roots, 'group', split_axis=0, concat_axis=0, tiled=True)  9.7 us
    unnamed x33, local copies, waits for them, and re-layouts  8.18 us
  transfers between devices with their start and end apart: 4, of which 0 were waited for; matrix products, arithmetic and copies ran while one was open for 11% of the time, Pallas kernels for 32%

commit v1 on v0

v1 whole, which is shorter than its diff:
```python
import functools

import jax
import jax.numpy as jnp
from jax import lax
from jax.experimental import pallas as pl
from jax.experimental.pallas import tpu as pltpu
from jax.sharding import PartitionSpec as P

f32 = jnp.float32
bf16 = jnp.bfloat16
highest = lax.Precision.HIGHEST

LEAF = 128
RANK = 32
RHS = 64
LEAVES = 32
PTS = 4096
NEAR = 27
HALO_L = 8
HALO = HALO_L * LEAF
WIN_L = LEAVES + 2 * HALO_L
WIN = WIN_L * LEAF
INTER = 8
GROUPS = 8
MEMBERS = 32
PATH = 5
FEATURES = 48

LOG2E = 1.4426950408889634
SCALE = LOG2E * 3.0**0.5 / 0.3
FLOOR = SCALE * SCALE * 1e-6
WEIGHT = 0.1 / LOG2E
DOWN = 2.0**0.5
VMEM_BYTES = 48 * 1024 * 1024

vmem = pl.BlockSpec(memory_space=pltpu.VMEM)
smem = pl.BlockSpec(memory_space=pltpu.SMEM)


def block(index, size):
    return pl.ds(pl.multiple_of(index * size, size), size)


def dot(a, b):
    return jnp.dot(a, b, precision=highest, preferred_element_type=f32)


def left_half(shape):
    return lax.broadcasted_iota(jnp.int32, shape, len(shape) - 1) < RHS


def swap(x):
    return pltpu.roll(x, RHS, 1)


def both(x):
    return jnp.where(left_half(x.shape), x, swap(x))


def fold(x):
    half = RANK // 2
    return jnp.where(left_half((half, 2 * RHS)), x[:half], swap(x[half:]))


def unfold(x):
    return jnp.concatenate([x, swap(x)], axis=0)


def two(x):
    high = x.astype(bf16)
    return high, (x - high.astype(f32)).astype(bf16)


def three(x):
    high = x.astype(bf16).astype(f32)
    rest = x - high
    middle = rest.astype(bf16).astype(f32)
    return high, middle, rest - middle


def spread(rows, ref, first):
    for c in range(RANK // 4):
        tile = rows[:, c * LEAF : (c + 1) * LEAF]
        for k in range(4):
            turned = tile if k == 0 else pltpu.roll(tile, LEAF - RANK * k, 1)
            ref[pl.ds(first * RANK + 4 * c + k, 8, stride=RANK), :] = turned


def matrix(ref, index):
    return ref[block(index, RANK), :RANK]


def spread_all(source_ref, ref, count):
    for first in range(0, count - 7, 8):
        spread(source_ref[first : first + 8, :], ref, first)
    if count % 8:
        spread(source_ref[count - 8 : count, :], ref, count - 8)


def spread_path(position, group_ref, rows_ref, ref):
    offset, count = 0, MEMBERS
    for i in range(8):
        if i < PATH:
            row = group_ref[pl.ds(offset + lax.shift_right_logical(position, i), 1), :]
            offset, count = offset + count, count // 2
        rows_ref[i : i + 1, :] = row
    spread(rows_ref[...], ref, 0)


def order_kernel(
    order_ref, charges_ref, coords_ref, basis_ref,
    points_ref, first_ref, last_ref, coef_ref,
    turned_ref, rows_ref, padded_ref,
):
    padded_ref[...] = jnp.zeros_like(padded_ref)
    padded_ref[0:3, :] = coords_ref[...]

    def turn(b, carry):
        columns = block(b, LEAF)
        tall = jnp.concatenate(
            [charges_ref[:, columns], padded_ref[:, columns], jnp.zeros((56, LEAF), f32)], axis=0
        )
        turned_ref[columns, :] = tall.T
        return carry

    lax.fori_loop(0, LEAVES, turn, 0, unroll=4)

    def fetch(b, carry):
        for i in range(64):
            at = b * 64 + i
            rows_ref[pl.ds(at, 1), :] = turned_ref[pl.ds(order_ref[0, at], 1), :]
        return carry

    lax.fori_loop(0, PTS // 64, fetch, 0)

    def coefficient(l, carry):
        columns = block(l, LEAF)
        rows = rows_ref[columns, :]
        high, low = two(rows)
        basis_high, basis_low = two(basis_ref[:, columns])
        y = jnp.dot(
            jnp.concatenate([basis_high, basis_low], axis=0),
            jnp.concatenate([high, low], axis=1),
            preferred_element_type=f32,
        )
        y = y[:RANK, : 2 * RHS] + y[:RANK, 2 * RHS :] + y[RANK:, : 2 * RHS]
        coef_ref[l] = both(y)
        points_ref[:, columns] = rows.T[: RHS + 8]
        return carry

    lax.fori_loop(0, LEAVES, coefficient, 0, unroll=4)

    first_ref[...] = points_ref[:, :HALO]
    last_ref[...] = points_ref[:, PTS - HALO :]


def up_kernel(
    place_ref, send_ref, coef_ref, local_in_ref, group_ref,
    sent_ref, level_ref, local_ref, path_in_ref, path_ref,
):
    spread_all(local_in_ref, local_ref, 2 * LEAVES - 2)
    spread_path(place_ref[0], group_ref, path_in_ref, path_ref)
    level_ref[...] = coef_ref[...]
    offset, count = 0, LEAVES
    while count > 1:
        values = [
            dot(matrix(local_ref, offset + 2 * i), level_ref[2 * i])
            + dot(matrix(local_ref, offset + 2 * i + 1), level_ref[2 * i + 1])
            for i in range(count // 2)
        ]
        for i, value in enumerate(values):
            level_ref[i] = value
        offset, count = offset + count, count // 2
    value = level_ref[0]
    for i in range(PATH):
        value = dot(matrix(path_ref, i), value)
    packed = fold(value)
    left = left_half((RANK, 2 * RHS))

    def pack(d, carry):
        for q in range(4):
            one = coef_ref[send_ref[0, d * 8 + 2 * q]]
            other = coef_ref[send_ref[0, d * 8 + 2 * q + 1]]
            sent_ref[d, q * RANK : (q + 1) * RANK, :] = jnp.where(left, one, other)
        sent_ref[d, 4 * RANK :, :] = packed
        return carry

    lax.fori_loop(0, MEMBERS, pack, 0, unroll=4)


def near_kernel(
    list_ref, points_ref, before_ref, after_ref,
    out_ref, target_ref, source_ref, weight_ref,
):
    row = lax.broadcasted_iota(jnp.int32, (8, LEAF), 0)
    zero = jnp.zeros((8, LEAF), f32)

    def prepare(w, x, own):
        columns = block(w, LEAF)
        weight_ref[:, columns] = jnp.concatenate(two(x[:RHS] * WEIGHT), axis=0)
        c = jnp.where(row < 3, (x[RHS:] - 0.5) * SCALE, 0.0)
        squares = jnp.sum(c * c, axis=0, keepdims=True) + 0.5 * FLOOR
        parts = three(jnp.broadcast_to(squares, (8, LEAF)))
        h, m, l = three(c)
        norm = jnp.where(row == 3, parts[0], jnp.where(row == 4, parts[1], parts[2]))
        is_norm = jnp.logical_and(row >= 3, row < 6)
        norm = jnp.where(is_norm, norm, 0.0)
        ones = jnp.where(is_norm, 1.0, 0.0)
        source = jnp.concatenate([h + ones, m + norm, l, h, m, h] + [zero] * 10, axis=0)
        source_ref[columns, :] = source.T[:, :FEATURES].astype(bf16)
        if own:
            target = jnp.concatenate(
                [-2.0 * h + norm, -2.0 * h + ones, -2.0 * h, -2.0 * m, -2.0 * m, -2.0 * l], axis=0
            )
            target_ref[:, block(w - HALO_L, LEAF)] = target.astype(bf16)

    def own(b, carry):
        prepare(b + HALO_L, points_ref[:, block(b, LEAF)], True)
        return carry

    lax.fori_loop(0, LEAVES, own, 0, unroll=4)
    for i in range(HALO_L):
        columns = slice(i * LEAF, (i + 1) * LEAF)
        prepare(i, before_ref[:, columns], False)
        prepare(HALO_L + LEAVES + i, after_ref[:, columns], False)

    def leaf(a, carry):
        columns = block(a, LEAF)
        target = target_ref[:, columns]
        at = [block(list_ref[a, j], LEAF) for j in range(NEAR)]
        source = jnp.concatenate([source_ref[s, :] for s in at], axis=0)
        weight = jnp.concatenate([weight_ref[:, s] for s in at], axis=1)
        squared = jnp.dot(source, target, preferred_element_type=f32)
        parts = []
        for j in range(NEAR):
            r = jnp.maximum(squared[j * LEAF : (j + 1) * LEAF], FLOOR)
            t = r * lax.rsqrt(r)
            parts.append(jnp.concatenate(two((t + LOG2E) * jnp.exp2(-t)), axis=1))
        total = jnp.dot(weight, jnp.concatenate(parts, axis=0), preferred_element_type=f32)
        out_ref[:, columns] = total[:RHS, :LEAF] + total[RHS:, :LEAF] + total[:RHS, LEAF:]
        return carry

    lax.fori_loop(0, LEAVES, leaf, 0, unroll=4)


def weights_kernel(
    place_ref, coupling_in_ref, local_in_ref, group_ref, basis_ref,
    coupling_ref, wide_basis_ref, wide_ref, local_ref, path_in_ref, path_ref,
):
    spread_all(local_in_ref, local_ref, 2 * LEAVES - 2)
    spread_path(place_ref[0], group_ref, path_in_ref, path_ref)

    def leaf(a, carry):
        spread(coupling_in_ref[block(a, INTER), :], wide_ref, a * INTER)
        return carry

    lax.fori_loop(0, LEAVES, leaf, 0, unroll=2)

    def join(a, carry):
        joined = jnp.concatenate([matrix(wide_ref, a * INTER + j) for j in range(INTER)], axis=1)
        coupling_ref[a] = jnp.concatenate(two(joined), axis=0)
        return carry

    lax.fori_loop(0, LEAVES, join, 0, unroll=2)

    node = matrix(path_ref, 0)
    for i in range(1, PATH):
        node = dot(matrix(path_ref, i), node)
    nodes = [node]
    offset = 2 * LEAVES - 4
    while len(nodes) < LEAVES:
        nodes = [
            dot(node, matrix(local_ref, offset + 2 * i + k))
            for i, node in enumerate(nodes)
            for k in (0, 1)
        ]
        offset = offset - 2 * len(nodes)
    gain = DOWN ** (2 * PATH)
    for i, node in enumerate(nodes):
        columns = slice(i * LEAF, (i + 1) * LEAF)
        carried = gain * dot(node, basis_ref[:, columns])
        wide_basis_ref[:, columns] = jnp.concatenate(two(carried), axis=0)


def root_kernel(slots_ref, out_ref, parts_ref, sem):
    copy = pltpu.make_async_copy(slots_ref.at[:, 4 * RANK :, :], parts_ref, sem)
    copy.start()
    copy.wait()
    packed = jnp.sum(parts_ref[...], axis=0)
    for g in range(GROUPS):
        out_ref[g] = packed


def turned_parts(x):
    high = x.astype(bf16).astype(f32)
    stacked = jnp.concatenate([high, x - high, high, jnp.zeros_like(high)], axis=0)
    return stacked.T.astype(bf16)


def far_kernel(recv_ref, slots_ref, coupling_ref, basis_ref, near_ref, out_ref):
    left = left_half((RANK, 2 * RHS))

    def far(a):
        picked = []
        for j in range(INTER):
            slot = recv_ref[0, a * INTER + j]
            use_left = (slot & 1) == 0
            rows = block(lax.shift_right_logical(slot, 1) & 3, RANK)
            picked.append(
                jnp.where(left == use_left, slots_ref[lax.shift_right_logical(slot, 3), rows, :], 0.0)
            )
        high, low = two(jnp.concatenate(picked, axis=0))
        y = jnp.dot(
            coupling_ref[a], jnp.concatenate([high, low], axis=1), preferred_element_type=f32
        )
        y = y[:RANK, : 2 * RHS] + y[:RANK, 2 * RHS :] + y[RANK:, : 2 * RHS]
        return y + swap(y)

    def finish(i, carry):
        turned = turned_parts(jnp.where(left, far(2 * i), far(2 * i + 1)))
        for k in (0, 1):
            columns = block(2 * i + k, LEAF)
            basis_high, basis_low = two(basis_ref[:, columns])
            basis = jnp.concatenate([basis_high, basis_high, basis_low, basis_low], axis=0)
            y = jnp.dot(turned[RHS * k : RHS * (k + 1)], basis, preferred_element_type=f32)
            out_ref[:, columns] = near_ref[:, columns] + y
        return carry

    lax.fori_loop(0, LEAVES // 2, finish, 0, unroll=4)


def final_kernel(roots_ref, top_ref, wide_basis_ref, partial_ref, out_ref):
    stacked = jnp.concatenate([unfold(roots_ref[g]) for g in range(GROUPS)], axis=0)
    turned = turned_parts(dot(top_ref[0], stacked))[:RHS]
    for start in range(0, PTS, 512):
        columns = slice(start, start + 512)
        high, low = wide_basis_ref[:RANK, columns], wide_basis_ref[RANK:, columns]
        basis = jnp.concatenate([high, high, low, low], axis=0)
        y = jnp.dot(turned, basis, preferred_element_type=f32)
        out_ref[:, columns] = partial_ref[:, columns] + y


def call(kernel, name, outs, specs, scratch, kind=f32):
    return pl.pallas_call(
        kernel,
        name=name,
        out_shape=[jax.ShapeDtypeStruct(s, kind) for s in outs],
        in_specs=specs,
        out_specs=[vmem] * len(outs),
        scratch_shapes=scratch,
        compiler_params=pltpu.CompilerParams(vmem_limit_bytes=VMEM_BYTES),
        cost_estimate=pl.CostEstimate(flops=10**9, bytes_accessed=2**20, transcendentals=0),
    )


def shards(
    charges,
    coords,
    point_order,
    near_list,
    send_list,
    recv_list,
    leaf_basis,
    local_transfer,
    leaf_coupling,
    group_transfer,
    top_coupling,
):
    place = lax.axis_index("dev").astype(jnp.int32).reshape(1)
    wide = [
        pltpu.VMEM(((2 * LEAVES - 2) * RANK, LEAF), f32),
        pltpu.VMEM((8, RANK * RANK), f32),
        pltpu.VMEM((8 * RANK, LEAF), f32),
    ]
    points, first, last, coef = call(
        order_kernel,
        "order",
        [(RHS + 8, PTS), (RHS + 8, HALO), (RHS + 8, HALO), (LEAVES, RANK, 2 * RHS)],
        [smem] + [vmem] * 3,
        [
            pltpu.VMEM((PTS, LEAF), f32),
            pltpu.VMEM((PTS, LEAF), f32),
            pltpu.VMEM((8, PTS), f32),
        ],
    )(point_order, charges, coords, leaf_basis)
    (sent,) = call(
        up_kernel,
        "up",
        [(MEMBERS, 4 * RANK + 16, 2 * RHS)],
        [smem] * 2 + [vmem] * 3,
        [pltpu.VMEM((LEAVES, RANK, 2 * RHS), f32)] + wide,
    )(place, send_list, coef, local_transfer, group_transfer)
    size = lax.axis_size("group") * lax.axis_size("dev")
    up = [(i, i + 1) for i in range(size - 1)]
    back = [(i + 1, i) for i in range(size - 1)]
    before = lax.ppermute(last, ("group", "dev"), up)
    after = lax.ppermute(first, ("group", "dev"), back)
    sent, before, after = lax.optimization_barrier((sent, before, after))
    slots = lax.all_to_all(sent, "dev", split_axis=0, concat_axis=0, tiled=True)
    (near,) = call(
        near_kernel,
        "near",
        [(RHS, PTS)],
        [smem, vmem, vmem, vmem],
        [
            pltpu.VMEM((FEATURES, PTS), bf16),
            pltpu.VMEM((WIN, FEATURES), bf16),
            pltpu.VMEM((2 * RHS, WIN), bf16),
        ],
    )(near_list, points, before, after)

    coupling, wide_basis = call(
        weights_kernel,
        "weights",
        [(LEAVES, 2 * RANK, INTER * RANK), (2 * RANK, PTS)],
        [smem] + [vmem] * 4,
        [pltpu.VMEM((LEAVES * INTER * RANK, LEAF), f32)] + wide,
        bf16,
    )(place, leaf_coupling, local_transfer, group_transfer, leaf_basis)
    (roots,) = call(
        root_kernel,
        "root",
        [(GROUPS, RANK // 2, 2 * RHS)],
        [pl.BlockSpec(memory_space=pl.ANY)],
        [pltpu.VMEM((MEMBERS, RANK // 2, 2 * RHS), f32), pltpu.SemaphoreType.DMA],
    )(slots)
    roots, slots = lax.optimization_barrier((roots, slots))
    roots = lax.all_to_all(roots, "group", split_axis=0, concat_axis=0, tiled=True)
    (partial,) = call(
        far_kernel, "far", [(RHS, PTS)], [smem] + [vmem] * 4, []
    )(recv_list, slots, coupling, leaf_basis, near)
    (potential,) = call(
        final_kernel, "final", [(RHS, PTS)], [vmem] * 4, []
    )(roots, top_coupling, wide_basis, partial)
    return potential


def solution(mesh):
    return jax.shard_map(
        shards,
        mesh=mesh,
        in_specs=(
            P(None, ("group", "dev")),
            P(None, ("group", "dev")),
            P(("group", "dev"), None),
            P(("group", "dev"), None),
            P(("group", "dev"), None),
            P(("group", "dev"), None),
            P(None, ("group", "dev")),
            P(("group", "dev"), None),
            P(("group", "dev"), None),
            P("group", None),
            P("group", None, None),
        ),
        out_specs=P(None, ("group", "dev")),
        check_vma=False,
    )
```

time: 156 us -> 118 us (0.76)
  Pallas kernels: 85.8 us -> 56.6 us
  waiting for transfers between devices: 0.01 us -> 13.2 us
  blocking collectives: 9.7 us -> 0 us
  local copies, waits for them, and re-layouts: 31.4 us -> 22.2 us
  starting transfers between devices: 26.6 us -> 23.5 us
    pallas_call x5 -> x7, Pallas kernels: 85.8 us -> 56.6 us  [the longest x1 28.2 us: shards(): call(near_kernel, 'near', [(RHS, PTS)], [smem, vmem, vmem, vmem], [pltpu....]
    reshape x9 -> x0, local copies, waits for them, and re-layouts: 23.2 us -> none  [the longest x2 11.9 us: shards(): leaf_coupling.reshape(LEAVES, INTER, RANK, RANK)]
    unnamed x33 -> x60, local copies, waits for them, and re-layouts: 8.18 us -> 22.2 us
    all_to_all x1, waiting for transfers between devices: 0.01 us -> 13.2 us  [shards(): slots = lax.all_to_all(sent, 'dev', split_axis=0, concat_axis=0, tiled=True)]
    all_to_all x1 -> x0, blocking collectives: 9.7 us -> none  [shards(): lax.all_to_all(roots, 'group', split_axis=0, concat_axis=0, tiled=True)]
    all_to_all x1, starting transfers between devices: 11.2 us -> 4.93 us  [shards(): lax.all_to_all(roots, 'group', split_axis=0, concat_axis=0, tiled=True)]
    all_to_all x1, starting transfers between devices: 10.2 us -> 13.3 us  [shards(): slots = lax.all_to_all(sent, 'dev', split_axis=0, concat_axis=0, tiled=True)]
  transfers between devices with their start and end apart: 4 -> 4, of which waited for: 0 -> 1; matrix products, arithmetic and copies ran while one was open for 11% -> 0% of each run, Pallas kernels for 32% -> 40%
where the time goes in v1:
time: 118 us; the launch traced here: 116 us
  Pallas kernels  56.6 us (48%)
  starting transfers between devices  23.5 us (20%)
  local copies, waits for them, and re-layouts  22.2 us (19%)
  waiting for transfers between devices  13.2 us (11%)
    pallas_call x1, Pallas kernels, shards(): call(near_kernel, 'near', [(RHS, PTS)], [smem, vmem, vmem, vmem], [pltpu....  28.2 us
    unnamed x60, local copies, waits for them, and re-layouts  22.2 us
    all_to_all x1, starting transfers between devices, shards(): slots = lax.all_to_all(sent, 'dev', split_axis=0, concat_axis=0, tiled=True)  13.3 us
    all_to_all x1, waiting for transfers between devices, shards(): slots = lax.all_to_all(sent, 'dev', split_axis=0, concat_axis=0, tiled=True)  13.2 us
    pallas_call x1, Pallas kernels, shards(): call(weights_kernel, 'weights', [(LEAVES, 2 * RANK, INTER * RANK), (2 * R...  8.21 us
    pallas_call x1, Pallas kernels, shards(): call(order_kernel, 'order', [(RHS + 8, PTS), (RHS + 8, HALO), (RHS + 8, H...  7.79 us
    pallas_call x1, Pallas kernels, shards(): call(far_kernel, 'far', [(RHS, PTS)], [smem] + [vmem] * 4, [])  6.37 us
    all_to_all x1, starting transfers between devices, shards(): lax.all_to_all(roots, 'group', split_axis=0, concat_axis=0, tiled=True)  4.93 us
  transfers between devices with their start and end apart: 4, of which 1 were waited for; matrix products, arithmetic and copies ran while one was open for 0% of the time, Pallas kernels for 40%

profile of v1, /device:TPU:17, one launch (start us, length us, event | category | flops | bytes accessed | tf_op | source)
XLA Modules:
  0.0 115.7 jit_solution(11598265989893122441)
XLA Ops:
  0.0 1.0 copy-done.5
  1.0 1.2 %copy-done.9 = f32[64,4096]{1,0:T(8,128)S(1)} copy-done((f32[64,4096]{1,0:T(8,128)S(1)}, f32[64,4096]{1,0:T(8,128)}, u32[]{:S(2)}) %copy-start.9) | copy-done | bytes 1048600
  2.3 0.8 copy-done.19
  3.1 0.7 copy-done.21
  3.8 7.8 %order.1 = (f32[72,4096]{1,0:T(8,128)S(1)}, f32[72,1024]{1,0:T(8,128)S(1)}, f32[72,1024]{1,0:T(8,128)S(1)}, f32[32,32,128]{2,1,0:T(8,128)S(1)}) custom-call(s32[1,4096]{1,0:T(1,128)S(1)} %copy-done.21, f32[64,4096]{1,0:T(8,128)S(1)} %copy-done.9, f32[3,4096]{1,0:T(4,128)S(1)} %copy-done.19, f32[32,4096]{1,0:T(8,128)S(1)} %copy-done.5), custom_call_target="tpu_custom_call" | custom-call | flops 1000000000 | bytes 1048576 | tf_op jit(solution)/shard_map/order/pallas_call | solution.py:376
  11.6 0.8 copy-done.24
  12.4 1.0 copy-done.26
  13.4 2.9 %collective-permute-start = (f32[72,1024]{1,0:T(8,128)S(1)}, f32[72,1024]{1,0:T(8,128)S(1)}, u32[]{:S(2)}, u32[]{:S(2)}) collective-permute-start(f32[72,1024]{1,0:T(8,128)S(1)} %get-tuple-element.17), channel_id=1, source_target_pairs={{0,1},{1,2},{2,3},{3,4},{4,5},{5,6},{6,7},{7,8},{8,9},{9,10},{10,1... | collective-permute-start | bytes 884744 | tf_op jit(solution)/shard_map/ppermute | solution.py:397
  16.3 2.4 %collective-permute-start.1 = (f32[72,1024]{1,0:T(8,128)S(1)}, f32[72,1024]{1,0:T(8,128)S(1)}, u32[]{:S(2)}, u32[]{:S(2)}) collective-permute-start(f32[72,1024]{1,0:T(8,128)S(1)} %get-tuple-element.18), channel_id=1, source_target_pairs={{1,0},{2,1},{3,2},{4,3},{5,4},{6,5},{7,6},{8,7},{9,8},{10,9},{11,1... | collective-permute-start | bytes 884744 | tf_op jit(solution)/shard_map/ppermute | solution.py:398
  18.8 0.9 copy-done.15
  19.7 0.9 copy-done.17
  20.6 1.0 copy-done.25
  21.7 3.7 %up.1 = f32[32,144,128]{2,1,0:T(8,128)S(1)} custom-call(s32[1]{0:T(128)} %bitcast.place_ref, s32[1,256]{1,0:T(1,128)S(1)} %copy-done.23, f32[32,32,128]{2,1,0:T(8,128)S(1)} %copy-done.25, f32[62,1024]{1,0:T(8,128)S(1)} %copy-done.15, f32[62,1024]{1,0:T(8,128)S(1)} %copy-done.17), custom_call_target="tpu_custom_call" | custom-call | flops 1000000000 | bytes 1048576 | tf_op jit(solution)/shard_map/up/pallas_call | solution.py:387
  25.4 1.4 %copy-done = f32[32,144,128]{2,1,0:T(8,128)} copy-done((f32[32,144,128]{2,1,0:T(8,128)}, f32[32,144,128]{2,1,0:T(8,128)S(1)}, u32[]{:S(2)}) %copy-start) | copy-done | bytes 2359320
  27.7 13.3 %all-to-all-start = ((f32[32,144,128]{2,1,0:T(8,128)}), f32[32,144,128]{2,1,0:T(8,128)S(1)}, u32[]{:S(2)}, u32[]{:S(2)}) async-start(f32[32,144,128]{2,1,0:T(8,128)} %copy-done), calls=%async_computation | async-start | bytes 4718592 | tf_op jit(solution)/shard_map/all_to_all | solution.py:400
  41.0 1.0 copy-done.6
  42.0 1.2 %copy-done.10 = f32[256,1024]{1,0:T(8,128)S(1)} copy-done((f32[256,1024]{1,0:T(8,128)S(1)}, f32[256,1024]{1,0:T(8,128)}, u32[]{:S(2)}) %copy-start.10) | copy-done | bytes 1048600
  43.3 0.9 copy-done.16
  44.2 0.9 copy-done.18
  45.2 8.2 %weights.1 = (bf16[32,64,256]{2,1,0:T(8,128)(2,1)S(1)}, bf16[64,4096]{1,0:T(8,128)(2,1)S(1)}) custom-call(s32[1]{0:T(128)} %bitcast.place_ref, f32[256,1024]{1,0:T(8,128)S(1)} %copy-done.10, f32[62,1024]{1,0:T(8,128)S(1)} %copy-done.16, f32[62,1024]{1,0:T(8,128)S(1)} %copy-done.18, f32[32,4096]{1,0:T(8,128)S(1)} %copy-done.6), custom_call_target="tpu_custom_call" | custom-call | flops 1000000000 | bytes 1048576 | tf_op jit(solution)/shard_map/weights/pallas_call | solution.py:413
  53.4 0.8 copy-done.28
  54.2 28.2 %near.1.near_ref = f32[64,4096]{1,0:T(8,128)S(1)} custom-call(s32[32,27]{1,0:T(8,128)S(1)} %copy-done.22, f32[72,4096]{1,0:T(8,128)S(1)} %copy-done.27, f32[72,1024]{1,0:T(8,128)S(1)} %copy-done.12, f32[72,1024]{1,0:T(8,128)S(1)} %copy-done.14), custom_call_target="tpu_custom_call" | custom-call | flops 1000000000 | bytes 1048576 | tf_op jit(solution)/shard_map/near/pallas_call | solution.py:401
  82.4 1.0 copy-done.1
  83.4 13.2 %all-to-all-done.slots_ref = f32[32,144,128]{2,1,0:T(8,128)S(1)} async-done(((f32[32,144,128]{2,1,0:T(8,128)}), f32[32,144,128]{2,1,0:T(8,128)S(1)}, u32[]{:S(2)}, u32[]{:S(2)}) %all-to-all-start) | async-done | bytes 2359328 | tf_op jit(solution)/shard_map/all_to_all | solution.py:400
  97.3 4.9 %all-to-all-start.1 = ((f32[8,16,128]{2,1,0:T(8,128)}), f32[8,16,128]{2,1,0:T(8,128)S(1)}, u32[]{:S(2)}, u32[]{:S(2)}) async-start(f32[8,16,128]{2,1,0:T(8,128)} %root.1), calls=%async_computation.1 | async-start | bytes 131072 | tf_op jit(solution)/shard_map/all_to_all | solution.py:429
  102.2 1.2 %copy-done.2 = f32[64,4096]{1,0:T(8,128)S(1)} copy-done((f32[64,4096]{1,0:T(8,128)S(1)}, f32[64,4096]{1,0:T(8,128)}, u32[]{:S(2)}) %copy-start.2) | copy-done | bytes 1048600
  103.5 1.0 copy-done.7
  104.5 6.4 %far.1.partial_ref = f32[64,4096]{1,0:T(8,128)S(1)} custom-call(s32[1,256]{1,0:T(1,128)S(1)} %copy-done.8, f32[32,144,128]{2,1,0:T(8,128)S(1)} %all-to-all-done.slots_ref, bf16[32,64,256]{2,1,0:T(8,128)(2,1)S(1)} %get-tuple-element.23.coupling_ref, f32[32,4096]{1,0:T(8,128)S(1)} %copy-done.7, f32[64,4096]{1,0:T(8,128)S(1)} %copy-done.2), custom_call_target="tpu_custom_call" | custom-call | flops 1000000000 | bytes 1048576 | tf_op jit(solution)/shard_map/far/pallas_call | solution.py:430
  110.9 1.0 copy-done.3
  111.9 1.2 %copy-done.4 = f32[64,4096]{1,0:T(8,128)S(1)} copy-done((f32[64,4096]{1,0:T(8,128)S(1)}, f32[64,4096]{1,0:T(8,128)}, u32[]{:S(2)}) %copy-start.4) | copy-done | bytes 1048600
  113.1 1.0 copy-done.29
  114.1 1.6 %final.1 = f32[64,4096]{1,0:T(8,128)} custom-call(f32[8,16,128]{2,1,0:T(8,128)S(1)} %all-to-all-done.1.roots_ref, f32[1,32,256]{2,1,0:T(8,128)S(1)} %copy-done.20, bf16[64,4096]{1,0:T(8,128)(2,1)S(1)} %copy-done.29, f32[64,4096]{1,0:T(8,128)S(1)} %copy-done.4), custom_call_target="tpu_custom_call" | custom-call | flops 1000000000 | bytes 1048576 | tf_op jit(solution)/shard_map/final/pallas_call | solution.py:433
  (43 shorter events, 1.6 us)
Async XLA Ops:
  0.0 1.0 copy-start.5
  1.0 1.2 %copy-start.9 = (f32[64,4096]{1,0:T(8,128)S(1)}, f32[64,4096]{1,0:T(8,128)}, u32[]{:S(2)}) copy-start(f32[64,4096]{1,0:T(8,128)} %charges_ref.1) | copy-start | bytes 3145732
  2.3 0.8 copy-start.19
  3.8 14.9 %copy-start.23 = (s32[1,256]{1,0:T(1,128)S(1)}, s32[1,256]{1,0:T(1,128)}, u32[]{:S(2)}) copy-start(s32[1,256]{1,0:T(1,128)} %send_ref.1) | copy-start | bytes 3076
  11.6 0.8 copy-start.24
  12.4 1.0 copy-start.26
  13.4 13.4 %collective-permute-start = (f32[72,1024]{1,0:T(8,128)S(1)}, f32[72,1024]{1,0:T(8,128)S(1)}, u32[]{:S(2)}, u32[]{:S(2)}) collective-permute-start(f32[72,1024]{1,0:T(8,128)S(1)} %get-tuple-element.17), channel_id=1, source_target_pairs={{0,1},{1,2},{2,3},{3,4},{4,5},{5,6},{6,7},{7,8},{8,9},{9,10},{10,1... | collective-permute-start | bytes 884744 | tf_op jit(solution)/shard_map/ppermute | solution.py:397
  16.3 10.5 %collective-permute-start.1 = (f32[72,1024]{1,0:T(8,128)S(1)}, f32[72,1024]{1,0:T(8,128)S(1)}, u32[]{:S(2)}, u32[]{:S(2)}) collective-permute-start(f32[72,1024]{1,0:T(8,128)S(1)} %get-tuple-element.18), channel_id=1, source_target_pairs={{1,0},{2,1},{3,2},{4,3},{5,4},{6,5},{7,6},{8,7},{9,8},{10,9},{11,1... | collective-permute-start | bytes 884744 | tf_op jit(solution)/shard_map/ppermute | solution.py:398
  18.7 1.0 copy-start.15
  19.7 0.9 copy-start.17
  20.6 1.0 copy-start.25
  25.4 1.4 %copy-start = (f32[32,144,128]{2,1,0:T(8,128)}, f32[32,144,128]{2,1,0:T(8,128)S(1)}, u32[]{:S(2)}) copy-start(f32[32,144,128]{2,1,0:T(8,128)S(1)} %up.1) | copy-start | bytes 7077892
  26.9 0.8 copy-start.13
  27.7 68.9 %all-to-all-start = ((f32[32,144,128]{2,1,0:T(8,128)}), f32[32,144,128]{2,1,0:T(8,128)S(1)}, u32[]{:S(2)}, u32[]{:S(2)}) async-start(f32[32,144,128]{2,1,0:T(8,128)} %copy-done), calls=%async_computation | async-start | bytes 4718592 | tf_op jit(solution)/shard_map/all_to_all | solution.py:400
  41.0 1.0 copy-start.6
  42.0 1.2 %copy-start.10 = (f32[256,1024]{1,0:T(8,128)S(1)}, f32[256,1024]{1,0:T(8,128)}, u32[]{:S(2)}) copy-start(f32[256,1024]{1,0:T(8,128)} %coupling_in_ref.1) | copy-start | bytes 3145732
  43.3 0.9 copy-start.16
  44.2 0.9 copy-start.18
  45.2 9.0 %copy-start.12 = (f32[72,1024]{1,0:T(8,128)S(1)}, f32[72,1024]{1,0:T(8,128)}, u32[]{:S(2)}) copy-start(f32[72,1024]{1,0:T(8,128)} %copy-done.11) | copy-start | bytes 884740
  45.2 9.0 %copy-start.14 = (f32[72,1024]{1,0:T(8,128)S(1)}, f32[72,1024]{1,0:T(8,128)}, u32[]{:S(2)}) copy-start(f32[72,1024]{1,0:T(8,128)} %copy-done.13) | copy-start | bytes 884740
  45.2 9.0 %copy-start.22 = (s32[32,27]{1,0:T(8,128)S(1)}, s32[32,27]{1,0:T(8,128)}, u32[]{:S(2)}) copy-start(s32[32,27]{1,0:T(8,128)} %list_ref.1) | copy-start | bytes 10372
  45.2 9.0 %copy-start.27 = (f32[72,4096]{1,0:T(8,128)S(1)}, f32[72,4096]{1,0:T(8,128)}, u32[]{:S(2)}) copy-start(f32[72,4096]{1,0:T(8,128)} %copy-done.26) | copy-start | bytes 3538948
  53.4 0.8 copy-start.28
  82.4 1.0 copy-start.1
  83.4 18.8 %copy-start.8 = (s32[1,256]{1,0:T(1,128)S(1)}, s32[1,256]{1,0:T(1,128)}, u32[]{:S(2)}) copy-start(s32[1,256]{1,0:T(1,128)} %recv_ref.1) | copy-start | bytes 3076
  97.3 14.6 %all-to-all-start.1 = ((f32[8,16,128]{2,1,0:T(8,128)}), f32[8,16,128]{2,1,0:T(8,128)S(1)}, u32[]{:S(2)}, u32[]{:S(2)}) async-start(f32[8,16,128]{2,1,0:T(8,128)} %root.1), calls=%async_computation.1 | async-start | bytes 131072 | tf_op jit(solution)/shard_map/all_to_all | solution.py:429
  102.2 1.2 %copy-start.2 = (f32[64,4096]{1,0:T(8,128)S(1)}, f32[64,4096]{1,0:T(8,128)}, u32[]{:S(2)}) copy-start(f32[64,4096]{1,0:T(8,128)} %copy-done.1) | copy-start | bytes 3145732
  103.5 1.0 copy-start.7
  104.5 7.4 %copy-start.20 = (f32[1,32,256]{2,1,0:T(8,128)S(1)}, f32[1,32,256]{2,1,0:T(8,128)}, u32[]{:S(2)}) copy-start(f32[1,32,256]{2,1,0:T(8,128)} %top_ref.1) | copy-start | bytes 98308
  110.9 1.0 copy-start.3
  111.9 1.2 %copy-start.4 = (f32[64,4096]{1,0:T(8,128)S(1)}, f32[64,4096]{1,0:T(8,128)}, u32[]{:S(2)}) copy-start(f32[64,4096]{1,0:T(8,128)} %copy-done.3) | copy-start | bytes 3145732
  113.1 1.0 copy-start.29
  (2 other events, 1.4 us)

commit v2 on v1

--- a/solution.py
+++ b/solution.py
@@ -32,9 +32,12 @@
 FLOOR = SCALE * SCALE * 1e-6
 WEIGHT = 0.1 / LOG2E
 DOWN = 2.0**0.5
-VMEM_BYTES = 48 * 1024 * 1024
+PART_L = HALO_L
+PARTS = [slice(HALO * i, HALO * (i + 1)) for i in range(PTS // HALO)]
+VMEM_BYTES = 60 * 1024 * 1024
 
 vmem = pl.BlockSpec(memory_space=pltpu.VMEM)
+hbm = pl.BlockSpec(memory_space=pl.ANY)
 smem = pl.BlockSpec(memory_space=pltpu.SMEM)
 
 
@@ -109,10 +112,20 @@
 
 
 def order_kernel(
-    order_ref, charges_ref, coords_ref, basis_ref,
-    points_ref, first_ref, last_ref, coef_ref,
-    turned_ref, rows_ref, padded_ref,
+    place_ref, order_ref, charges_hbm, coords_ref, basis_hbm, local_hbm, group_hbm,
+    points_hbm, first_hbm, last_hbm, coef_hbm, roots_hbm,
+    charges_ref, basis_ref, points_ref, coef_ref, turned_ref, rows_ref, padded_ref,
+    level_ref, roots_ref, local_in_ref, group_ref, local_ref, path_in_ref, path_ref,
+    sems, out_sems,
 ):
+    loads = [
+        pltpu.make_async_copy(charges_hbm.at[:, part], charges_ref.at[:, part], sems.at[i])
+        for i, part in enumerate(PARTS)
+    ]
+    for source, target in ((basis_hbm, basis_ref), (local_hbm, local_in_ref), (group_hbm, group_ref)):
+        loads.append(pltpu.make_async_copy(source, target, sems.at[len(loads)]))
+    for load in loads:
+        load.start()
     padded_ref[...] = jnp.zeros_like(padded_ref)
     padded_ref[0:3, :] = coords_ref[...]
 
@@ -124,7 +137,9 @@
         turned_ref[columns, :] = tall.T
         return carry
 
-    lax.fori_loop(0, LEAVES, turn, 0, unroll=4)
+    for i in range(len(PARTS)):
+        loads[i].wait()
+        lax.fori_loop(PART_L * i, PART_L * (i + 1), turn, 0, unroll=4)
 
     def fetch(b, carry):
         for i in range(64):
@@ -149,26 +164,36 @@
         points_ref[:, columns] = rows.T[: RHS + 8]
         return carry
 
-    lax.fori_loop(0, LEAVES, coefficient, 0, unroll=4)
-
-    first_ref[...] = points_ref[:, :HALO]
-    last_ref[...] = points_ref[:, PTS - HALO :]
-
-
-def up_kernel(
-    place_ref, send_ref, coef_ref, local_in_ref, group_ref,
-    sent_ref, level_ref, local_ref, path_in_ref, path_ref,
-):
+    for load in loads[len(PARTS) :]:
+        load.wait()
+    stores = []
+
+    def store(source, target):
+        copy = pltpu.make_async_copy(source, target, out_sems.at[len(stores)])
+        copy.start()
+        stores.append(copy)
+
+    for i, part in enumerate(PARTS):
+        lax.fori_loop(PART_L * i, PART_L * (i + 1), coefficient, 0, unroll=4)
+        leaves = slice(PART_L * i, PART_L * (i + 1))
+        store(coef_ref.at[leaves], coef_hbm.at[leaves])
+        store(points_ref.at[:, part], points_hbm.at[:, part])
+        if i == 0:
+            store(points_ref.at[:, part], first_hbm)
+        if i == len(PARTS) - 1:
+            store(points_ref.at[:, part], last_hbm)
+
     spread_all(local_in_ref, local_ref, 2 * LEAVES - 2)
     spread_path(place_ref[0], group_ref, path_in_ref, path_ref)
-    level_ref[...] = coef_ref[...]
+    nodes = coef_ref
     offset, count = 0, LEAVES
     while count > 1:
         values = [
-            dot(matrix(local_ref, offset + 2 * i), level_ref[2 * i])
-            + dot(matrix(local_ref, offset + 2 * i + 1), level_ref[2 * i + 1])
+            dot(matrix(local_ref, offset + 2 * i), nodes[2 * i])
+            + dot(matrix(local_ref, offset + 2 * i + 1), nodes[2 * i + 1])
             for i in range(count // 2)
         ]
+        nodes = level_ref
         for i, value in enumerate(values):
             level_ref[i] = value
         offset, count = offset + count, count // 2
@@ -176,17 +201,47 @@
     for i in range(PATH):
         value = dot(matrix(path_ref, i), value)
     packed = fold(value)
+    for g in range(GROUPS):
+        roots_ref[g] = packed
+    store(roots_ref, roots_hbm)
+    for copy in stores:
+        copy.wait()
+
+
+def top_kernel(roots_ref, top_ref, sent_in_hbm, sent_hbm, tops_ref, sem):
+    stacked = jnp.concatenate([unfold(roots_ref[g]) for g in range(GROUPS)], axis=0)
+    packed = fold(dot(top_ref[0], stacked))
+    for d in range(MEMBERS):
+        tops_ref[d] = packed
+    copy = pltpu.make_async_copy(tops_ref, sent_hbm.at[:, 4 * RANK :, :], sem)
+    copy.start()
+    copy.wait()
+
+
+def pack_kernel(send_ref, coef_hbm, sent_hbm, coef_ref, sent_ref, sems):
+    load = pltpu.make_async_copy(coef_hbm, coef_ref, sems.at[0])
+    load.start()
     left = left_half((RANK, 2 * RHS))
+    load.wait()
 
     def pack(d, carry):
         for q in range(4):
             one = coef_ref[send_ref[0, d * 8 + 2 * q]]
             other = coef_ref[send_ref[0, d * 8 + 2 * q + 1]]
             sent_ref[d, q * RANK : (q + 1) * RANK, :] = jnp.where(left, one, other)
-        sent_ref[d, 4 * RANK :, :] = packed
-        return carry
-
-    lax.fori_loop(0, MEMBERS, pack, 0, unroll=4)
+        return carry
+
+    stores = []
+    for i in range(4):
+        lax.fori_loop(8 * i, 8 * (i + 1), pack, 0, unroll=4)
+        some = slice(8 * i, 8 * (i + 1))
+        copy = pltpu.make_async_copy(
+            sent_ref.at[some], sent_hbm.at[some, : 4 * RANK, :], sems.at[i + 1]
+        )
+        copy.start()
+        stores.append(copy)
+    for copy in stores:
+        copy.wait()
 
 
 def near_kernel(
@@ -283,22 +338,37 @@
         wide_basis_ref[:, columns] = jnp.concatenate(two(carried), axis=0)
 
 
-def root_kernel(slots_ref, out_ref, parts_ref, sem):
-    copy = pltpu.make_async_copy(slots_ref.at[:, 4 * RANK :, :], parts_ref, sem)
-    copy.start()
-    copy.wait()
-    packed = jnp.sum(parts_ref[...], axis=0)
-    for g in range(GROUPS):
-        out_ref[g] = packed
-
-
 def turned_parts(x):
     high = x.astype(bf16).astype(f32)
     stacked = jnp.concatenate([high, x - high, high, jnp.zeros_like(high)], axis=0)
     return stacked.T.astype(bf16)
 
 
-def far_kernel(recv_ref, slots_ref, coupling_ref, basis_ref, near_ref, out_ref):
+def far_kernel(
+    recv_ref, slots_hbm, coupling_hbm, basis_hbm, wide_basis_hbm, near_hbm,
+    out_hbm, slots_ref, coupling_ref, basis_ref, wide_basis_ref, near_ref, turned_ref,
+    sems, out_sems,
+):
+    loads = [
+        pltpu.make_async_copy(source, target, sems.at[i])
+        for i, (source, target) in enumerate(
+            (
+                (slots_hbm, slots_ref),
+                (coupling_hbm, coupling_ref),
+                (basis_hbm, basis_ref),
+                (wide_basis_hbm, wide_basis_ref),
+                (near_hbm, near_ref),
+            )
+        )
+    ]
+    for load in loads:
+        load.start()
+    for load in loads[:2]:
+        load.wait()
+    top = slots_ref[0, 4 * RANK :, :]
+    for d in range(1, MEMBERS):
+        top = top + slots_ref[d, 4 * RANK :, :]
+    top = turned_parts(unfold(top))[:RHS]
     left = left_half((RANK, 2 * RHS))
 
     def far(a):
@@ -317,38 +387,46 @@
         y = y[:RANK, : 2 * RHS] + y[:RANK, 2 * RHS :] + y[RANK:, : 2 * RHS]
         return y + swap(y)
 
-    def finish(i, carry):
-        turned = turned_parts(jnp.where(left, far(2 * i), far(2 * i + 1)))
-        for k in (0, 1):
-            columns = block(2 * i + k, LEAF)
-            basis_high, basis_low = two(basis_ref[:, columns])
-            basis = jnp.concatenate([basis_high, basis_high, basis_low, basis_low], axis=0)
-            y = jnp.dot(turned[RHS * k : RHS * (k + 1)], basis, preferred_element_type=f32)
-            out_ref[:, columns] = near_ref[:, columns] + y
-        return carry
-
-    lax.fori_loop(0, LEAVES // 2, finish, 0, unroll=4)
-
-
-def final_kernel(roots_ref, top_ref, wide_basis_ref, partial_ref, out_ref):
-    stacked = jnp.concatenate([unfold(roots_ref[g]) for g in range(GROUPS)], axis=0)
-    turned = turned_parts(dot(top_ref[0], stacked))[:RHS]
-    for start in range(0, PTS, 512):
-        columns = slice(start, start + 512)
+    def turn(i, carry):
+        turned_ref[i] = turned_parts(jnp.where(left, far(2 * i), far(2 * i + 1)))
+        return carry
+
+    lax.fori_loop(0, LEAVES // 2, turn, 0, unroll=8)
+    for load in loads[2:]:
+        load.wait()
+
+    def finish(a, carry):
+        columns = block(a, LEAF)
+        basis_high, basis_low = two(basis_ref[:, columns])
         high, low = wide_basis_ref[:RANK, columns], wide_basis_ref[RANK:, columns]
-        basis = jnp.concatenate([high, high, low, low], axis=0)
-        y = jnp.dot(turned, basis, preferred_element_type=f32)
-        out_ref[:, columns] = partial_ref[:, columns] + y
-
-
-def call(kernel, name, outs, specs, scratch, kind=f32):
+        basis = jnp.concatenate(
+            [basis_high, basis_high, basis_low, basis_low, high, high, low, low], axis=0
+        )
+        rows = turned_ref[lax.shift_right_logical(a, 1), block(a & 1, RHS), :]
+        joined = jnp.concatenate([rows, top], axis=1)
+        y = jnp.dot(joined, basis, preferred_element_type=f32)
+        near_ref[:, columns] = near_ref[:, columns] + y
+        return carry
+
+    stores = []
+    for i, part in enumerate(PARTS):
+        lax.fori_loop(PART_L * i, PART_L * (i + 1), finish, 0, unroll=8)
+        copy = pltpu.make_async_copy(near_ref.at[:, part], out_hbm.at[:, part], out_sems.at[i])
+        copy.start()
+        stores.append(copy)
+    for copy in stores:
+        copy.wait()
+
+
+def call(kernel, name, outs, specs, scratch, kind=f32, out=vmem, aliases=None):
     return pl.pallas_call(
         kernel,
         name=name,
         out_shape=[jax.ShapeDtypeStruct(s, kind) for s in outs],
         in_specs=specs,
-        out_specs=[vmem] * len(outs),
+        out_specs=[out] * len(outs),
         scratch_shapes=scratch,
+        input_output_aliases=aliases or {},
         compiler_params=pltpu.CompilerParams(vmem_limit_bytes=VMEM_BYTES),
         cost_estimate=pl.CostEstimate(flops=10**9, bytes_accessed=2**20, transcendentals=0),
     )
@@ -373,30 +451,62 @@
         pltpu.VMEM((8, RANK * RANK), f32),
         pltpu.VMEM((8 * RANK, LEAF), f32),
     ]
-    points, first, last, coef = call(
+    points, first, last, coef, roots = call(
         order_kernel,
         "order",
-        [(RHS + 8, PTS), (RHS + 8, HALO), (RHS + 8, HALO), (LEAVES, RANK, 2 * RHS)],
-        [smem] + [vmem] * 3,
         [
+            (RHS + 8, PTS), (RHS + 8, HALO), (RHS + 8, HALO),
+            (LEAVES, RANK, 2 * RHS), (GROUPS, RANK // 2, 2 * RHS),
+        ],
+        [smem, smem, hbm, vmem, hbm, hbm, hbm],
+        [
+            pltpu.VMEM((RHS, PTS), f32),
+            pltpu.VMEM((RANK, PTS), f32),
+            pltpu.VMEM((RHS + 8, PTS), f32),
+            pltpu.VMEM((LEAVES, RANK, 2 * RHS), f32),
             pltpu.VMEM((PTS, LEAF), f32),
             pltpu.VMEM((PTS, LEAF), f32),
             pltpu.VMEM((8, PTS), f32),
+            pltpu.VMEM((LEAVES // 2, RANK, 2 * RHS), f32),
+            pltpu.VMEM((GROUPS, RANK // 2, 2 * RHS), f32),
+            pltpu.VMEM((2 * LEAVES - 2, RANK * RANK), f32),
+            pltpu.VMEM((2 * MEMBERS - 2, RANK * RANK), f32),
+        ]
+        + wide
+        + [
+            pltpu.SemaphoreType.DMA((len(PARTS) + 3,)),
+            pltpu.SemaphoreType.DMA((2 * len(PARTS) + 3,)),
         ],
-    )(point_order, charges, coords, leaf_basis)
+        out=hbm,
+    )(place, point_order, charges, coords, leaf_basis, local_transfer, group_transfer)
     (sent,) = call(
-        up_kernel,
-        "up",
-        [(MEMBERS, 4 * RANK + 16, 2 * RHS)],
-        [smem] * 2 + [vmem] * 3,
-        [pltpu.VMEM((LEAVES, RANK, 2 * RHS), f32)] + wide,
-    )(place, send_list, coef, local_transfer, group_transfer)
+        pack_kernel,
+        "pack",
+        [(MEMBERS, 4 * RANK + RANK // 2, 2 * RHS)],
+        [smem, hbm],
+        [
+            pltpu.VMEM((LEAVES, RANK, 2 * RHS), f32),
+            pltpu.VMEM((MEMBERS, 4 * RANK, 2 * RHS), f32),
+            pltpu.SemaphoreType.DMA((5,)),
+        ],
+        out=hbm,
+    )(send_list, coef)
+    roots = lax.all_to_all(roots, "group", split_axis=0, concat_axis=0, tiled=True)
     size = lax.axis_size("group") * lax.axis_size("dev")
     up = [(i, i + 1) for i in range(size - 1)]
     back = [(i + 1, i) for i in range(size - 1)]
     before = lax.ppermute(last, ("group", "dev"), up)
     after = lax.ppermute(first, ("group", "dev"), back)
-    sent, before, after = lax.optimization_barrier((sent, before, after))
+    roots, before, after = lax.optimization_barrier((roots, before, after))
+    (sent,) = call(
+        top_kernel,
+        "top",
+        [sent.shape],
+        [vmem, vmem, hbm],
+        [pltpu.VMEM((MEMBERS, RANK // 2, 2 * RHS), f32), pltpu.SemaphoreType.DMA],
+        out=hbm,
+        aliases={2: 0},
+    )(roots, top_coupling, sent)
     slots = lax.all_to_all(sent, "dev", split_axis=0, concat_axis=0, tiled=True)
     (near,) = call(
         near_kernel,
@@ -418,21 +528,23 @@
         [pltpu.VMEM((LEAVES * INTER * RANK, LEAF), f32)] + wide,
         bf16,
     )(place, leaf_coupling, local_transfer, group_transfer, leaf_basis)
-    (roots,) = call(
-        root_kernel,
-        "root",
-        [(GROUPS, RANK // 2, 2 * RHS)],
-        [pl.BlockSpec(memory_space=pl.ANY)],
-        [pltpu.VMEM((MEMBERS, RANK // 2, 2 * RHS), f32), pltpu.SemaphoreType.DMA],
-    )(slots)
-    roots, slots = lax.optimization_barrier((roots, slots))
-    roots = lax.all_to_all(roots, "group", split_axis=0, concat_axis=0, tiled=True)
-    (partial,) = call(
-        far_kernel, "far", [(RHS, PTS)], [smem] + [vmem] * 4, []
-    )(recv_list, slots, coupling, leaf_basis, near)
     (potential,) = call(
-        final_kernel, "final", [(RHS, PTS)], [vmem] * 4, []
-    )(roots, top_coupling, wide_basis, partial)
+        far_kernel,
+        "far",
+        [(RHS, PTS)],
+        [smem] + [hbm] * 5,
+        [
+            pltpu.VMEM((MEMBERS, 4 * RANK + RANK // 2, 2 * RHS), f32),
+            pltpu.VMEM((LEAVES, 2 * RANK, INTER * RANK), bf16),
+            pltpu.VMEM((RANK, PTS), f32),
+            pltpu.VMEM((2 * RANK, PTS), bf16),
+            pltpu.VMEM((RHS, PTS), f32),
+            pltpu.VMEM((LEAVES // 2, 2 * RHS, 2 * RHS), bf16),
+            pltpu.SemaphoreType.DMA((5,)),
+            pltpu.SemaphoreType.DMA((len(PARTS),)),
+        ],
+        out=hbm,
+    )(recv_list, slots, coupling, leaf_basis, wide_basis, near)
     return potential
 
 

time: 118 us -> 106 us (0.90); the launches traced: 116 us -> 106 us
  local copies, waits for them, and re-layouts: 22.2 us -> 2.02 us
  Pallas kernels: 56.6 us -> 63.8 us
  waiting for transfers between devices: 13.2 us -> 17.2 us
    unnamed x60 -> x8, local copies, waits for them, and re-layouts: 22.2 us -> 2.02 us
    pallas_call x1, Pallas kernels: 7.79 us -> 12.4 us  [shards(): call(order_kernel, 'order', [(RHS + 8, PTS), (RHS + 8, HALO), (RHS + 8, H...]
    all_to_all x1, waiting for transfers between devices: 13.2 us -> 15.6 us  [shards(): slots = lax.all_to_all(sent, 'dev', split_axis=0, concat_axis=0, tiled=True)]
    pallas_call x1, Pallas kernels: 8.21 us -> 10.4 us  [shards(): call(weights_kernel, 'weights', [(LEAVES, 2 * RANK, INTER * RANK), (2 * R...]
    pallas_call x1, Pallas kernels: 28.2 us -> 29.9 us  [shards(): call(near_kernel, 'near', [(RHS, PTS)], [smem, vmem, vmem, vmem], [pltpu....]
    all_to_all x1, waiting for transfers between devices: 0.01 us -> 1.62 us  [shards(): lax.all_to_all(roots, 'group', split_axis=0, concat_axis=0, tiled=True)]
    all_to_all x1, starting transfers between devices: 13.3 us -> 11.7 us  [shards(): slots = lax.all_to_all(sent, 'dev', split_axis=0, concat_axis=0, tiled=True)]
    pallas_call x4 -> x3, Pallas kernels: 12.4 us -> 11.1 us  [the longest x1 5.83 us: shards(): call(far_kernel, 'far', [(RHS, PTS)], [smem] + [hbm] * 5, [pltpu.VMEM((ME...]
  transfers between devices with their start and end apart: 4 -> 4, of which waited for: 1 -> 2; matrix products, arithmetic and copies ran while one was open for 0% -> 0% of each run, Pallas kernels for 40% -> 41%
where the time goes in v2:
time: 106 us
  Pallas kernels  63.8 us (60%)
  starting transfers between devices  22.6 us (21%)
  waiting for transfers between devices  17.2 us (16%)
  local copies, waits for them, and re-layouts  2.02 us (2%)
    pallas_call x1, Pallas kernels, shards(): call(near_kernel, 'near', [(RHS, PTS)], [smem, vmem, vmem, vmem], [pltpu....  29.9 us
    all_to_all x1, waiting for transfers between devices, shards(): slots = lax.all_to_all(sent, 'dev', split_axis=0, concat_axis=0, tiled=True)  15.6 us
    pallas_call x1, Pallas kernels, shards(): call(order_kernel, 'order', [(RHS + 8, PTS), (RHS + 8, HALO), (RHS + 8, H...  12.4 us
    all_to_all x1, starting transfers between devices, shards(): slots = lax.all_to_all(sent, 'dev', split_axis=0, concat_axis=0, tiled=True)  11.7 us
    pallas_call x1, Pallas kernels, shards(): call(weights_kernel, 'weights', [(LEAVES, 2 * RANK, INTER * RANK), (2 * R...  10.4 us
    pallas_call x1, Pallas kernels, shards(): call(far_kernel, 'far', [(RHS, PTS)], [smem] + [hbm] * 5, [pltpu.VMEM((ME...  5.83 us
    all_to_all x1, starting transfers between devices, shards(): lax.all_to_all(roots, 'group', split_axis=0, concat_axis=0, tiled=True)  5.54 us
    pallas_call x1, Pallas kernels, shards(): call(pack_kernel, 'pack', [(MEMBERS, 4 * RANK + RANK // 2, 2 * RHS)], [sm...  3.22 us
  transfers between devices with their start and end apart: 4, of which 2 were waited for; matrix products, arithmetic and copies ran while one was open for 0% of the time, Pallas kernels for 41%

profile of v2, /device:TPU:17, one launch (start us, length us, event | category | flops | bytes accessed | tf_op | source)
XLA Modules:
  0.0 105.7 jit_solution(14598726596056813097)
XLA Ops:
  0.0 12.4 %order.1 = (f32[72,4096]{1,0:T(8,128)}, f32[72,1024]{1,0:T(8,128)}, f32[72,1024]{1,0:T(8,128)}, f32[32,32,128]{2,1,0:T(8,128)}, f32[8,16,128]{2,1,0:T(8,128)}) custom-call(s32[1]{0:T(128)} %bitcast.place_ref, s32[1,4096]{1,0:T(1,128)} %order_ref.1, f32[64,4096]{1,0:T(8,128)} %charges_hbm.1, f32[3,4096]{1,0:T(4,128)} %coords_ref.1, f32[32,4096]{1,0:T(8,128)} %basis_hbm.3, ...), custom_call_target="tpu_custom_call" | custom-call | flops 1000000000 | bytes 1048576 | tf_op jit(solution)/shard_map/order/pallas_call | solution.py:454
  12.4 2.9 %collective-permute-start = (f32[72,1024]{1,0:T(8,128)}, f32[72,1024]{1,0:T(8,128)S(1)}, u32[]{:S(2)}, u32[]{:S(2)}) collective-permute-start(f32[72,1024]{1,0:T(8,128)} %get-tuple-element.16), channel_id=1, source_target_pairs={{0,1},{1,2},{2,3},{3,4},{4,5},{5,6},{6,7},{7,8},{8,9},{9,10},{10,1... | collective-permute-start | bytes 884744 | tf_op jit(solution)/shard_map/ppermute | solution.py:498
  15.3 2.4 %collective-permute-start.1 = (f32[72,1024]{1,0:T(8,128)}, f32[72,1024]{1,0:T(8,128)S(1)}, u32[]{:S(2)}, u32[]{:S(2)}) collective-permute-start(f32[72,1024]{1,0:T(8,128)} %get-tuple-element.17), channel_id=1, source_target_pairs={{1,0},{2,1},{3,2},{4,3},{5,4},{6,5},{7,6},{8,7},{9,8},{10,9},{11,1... | collective-permute-start | bytes 884744 | tf_op jit(solution)/shard_map/ppermute | solution.py:499
  17.7 5.5 %all-to-all-start = ((f32[8,16,128]{2,1,0:T(8,128)}), f32[8,16,128]{2,1,0:T(8,128)S(1)}, u32[]{:S(2)}, u32[]{:S(2)}) async-start(f32[8,16,128]{2,1,0:T(8,128)} %get-tuple-element.15), calls=%async_computation | async-start | bytes 131072 | tf_op jit(solution)/shard_map/all_to_all | solution.py:494
  23.2 3.2 %pack.1.sent_in_hbm = f32[32,144,128]{2,1,0:T(8,128)} custom-call(s32[1,256]{1,0:T(1,128)} %send_ref.1, f32[32,32,128]{2,1,0:T(8,128)} %get-tuple-element.19.coef_hbm), custom_call_target="tpu_custom_call" | custom-call | flops 1000000000 | bytes 1048576 | tf_op jit(solution)/shard_map/pack/pallas_call | solution.py:482
  26.5 1.6 %all-to-all-done.roots_ref = f32[8,16,128]{2,1,0:T(8,128)S(1)} async-done(((f32[8,16,128]{2,1,0:T(8,128)}), f32[8,16,128]{2,1,0:T(8,128)S(1)}, u32[]{:S(2)}, u32[]{:S(2)}) %all-to-all-start) | async-done | bytes 65568 | tf_op jit(solution)/shard_map/all_to_all | solution.py:494
  28.1 0.0 copy-start.1
  28.1 0.0 collective-permute-done.before_ref
  28.1 0.0 copy-start.2
  28.1 0.0 collective-permute-done.1.after_ref
  28.1 0.6 copy-done.1
  28.7 0.0 copy-start.3
  28.7 2.0 %top.1 = f32[32,144,128]{2,1,0:T(8,128)} custom-call(f32[8,16,128]{2,1,0:T(8,128)} %copy-done.1, f32[1,32,256]{2,1,0:T(8,128)} %top_ref.1, f32[32,144,128]{2,1,0:T(8,128)} %pack.1.sent_in_hbm), custom_call_target="tpu_custom_call", output_to_operand_aliasing={{}: (2, {})} | custom-call | flops 1000000000 | bytes 1048576 | tf_op jit(solution)/shard_map/top/pallas_call | solution.py:501
  30.7 0.0 copy-done.2
  30.8 0.0 copy-done.3
  30.8 11.7 %all-to-all-start.1 = ((f32[32,144,128]{2,1,0:T(8,128)}), f32[32,144,128]{2,1,0:T(8,128)S(1)}, u32[]{:S(2)}, u32[]{:S(2)}) async-start(f32[32,144,128]{2,1,0:T(8,128)} %top.1), calls=%async_computation.1 | async-start | bytes 4718592 | tf_op jit(solution)/shard_map/all_to_all | solution.py:510
  42.5 10.4 %weights.1 = (bf16[32,64,256]{2,1,0:T(8,128)(2,1)}, bf16[64,4096]{1,0:T(8,128)(2,1)}) custom-call(s32[1]{0:T(128)} %bitcast.place_ref, f32[256,1024]{1,0:T(8,128)} %coupling_in_ref.1, f32[62,1024]{1,0:T(8,128)} %local_in_ref.1, f32[62,1024]{1,0:T(8,128)} %group_ref.1, f32[32,4096]{1,0:T(8,128)} %basis_hbm.3), custom_call_target="tpu_custom_call" | custom-call | flops 1000000000 | bytes 1048576 | tf_op jit(solution)/shard_map/weights/pallas_call | solution.py:523
  52.9 29.9 %near.1.near_hbm = f32[64,4096]{1,0:T(8,128)} custom-call(s32[32,27]{1,0:T(8,128)} %list_ref.1, f32[72,4096]{1,0:T(8,128)} %get-tuple-element.22.points_ref, f32[72,1024]{1,0:T(8,128)} %copy-done.2, f32[72,1024]{1,0:T(8,128)} %copy-done.3), custom_call_target="tpu_custom_call" | custom-call | flops 1000000000 | bytes 1048576 | tf_op jit(solution)/shard_map/near/pallas_call | solution.py:511
  82.8 15.6 %all-to-all-done.1.slots_hbm = f32[32,144,128]{2,1,0:T(8,128)S(1)} async-done(((f32[32,144,128]{2,1,0:T(8,128)}), f32[32,144,128]{2,1,0:T(8,128)S(1)}, u32[]{:S(2)}, u32[]{:S(2)}) %all-to-all-start.1) | async-done | bytes 2359328 | tf_op jit(solution)/shard_map/all_to_all | solution.py:510
  98.4 0.0 copy-start
  98.4 1.4 %copy-done = f32[32,144,128]{2,1,0:T(8,128)} copy-done((f32[32,144,128]{2,1,0:T(8,128)}, f32[32,144,128]{2,1,0:T(8,128)S(1)}, u32[]{:S(2)}) %copy-start) | copy-done | bytes 2359320
  99.8 5.8 %far.1 = f32[64,4096]{1,0:T(8,128)} custom-call(s32[1,256]{1,0:T(1,128)} %recv_ref.1, f32[32,144,128]{2,1,0:T(8,128)} %copy-done, bf16[32,64,256]{2,1,0:T(8,128)(2,1)} %get-tuple-element.20.coupling_hbm, f32[32,4096]{1,0:T(8,128)} %basis_hbm.3, bf16[64,4096]{1,0:T(8,128)(2,1)} %get-tuple-element.21.wide_basis_hbm, f32[64,4096]{1,0:T(8,128)} %near.1.near_hbm), custom_call_target="tpu_custom_call" | custom-call | flops 1000000000 | bytes 1048576 | tf_op jit(solution)/shard_map/far/pallas_call | solution.py:531
Async XLA Ops:
  12.4 15.7 %collective-permute-start = (f32[72,1024]{1,0:T(8,128)}, f32[72,1024]{1,0:T(8,128)S(1)}, u32[]{:S(2)}, u32[]{:S(2)}) collective-permute-start(f32[72,1024]{1,0:T(8,128)} %get-tuple-element.16), channel_id=1, source_target_pairs={{0,1},{1,2},{2,3},{3,4},{4,5},{5,6},{6,7},{7,8},{8,9},{9,10},{10,1... | collective-permute-start | bytes 884744 | tf_op jit(solution)/shard_map/ppermute | solution.py:498
  15.3 12.8 %collective-permute-start.1 = (f32[72,1024]{1,0:T(8,128)}, f32[72,1024]{1,0:T(8,128)S(1)}, u32[]{:S(2)}, u32[]{:S(2)}) collective-permute-start(f32[72,1024]{1,0:T(8,128)} %get-tuple-element.17), channel_id=1, source_target_pairs={{1,0},{2,1},{3,2},{4,3},{5,4},{6,5},{7,6},{8,7},{9,8},{10,9},{11,1... | collective-permute-start | bytes 884744 | tf_op jit(solution)/shard_map/ppermute | solution.py:499
  17.7 10.4 %all-to-all-start = ((f32[8,16,128]{2,1,0:T(8,128)}), f32[8,16,128]{2,1,0:T(8,128)S(1)}, u32[]{:S(2)}, u32[]{:S(2)}) async-start(f32[8,16,128]{2,1,0:T(8,128)} %get-tuple-element.15), calls=%async_computation | async-start | bytes 131072 | tf_op jit(solution)/shard_map/all_to_all | solution.py:494
  28.1 0.6 copy-start.1
  28.1 2.6 %copy-start.2 = (f32[72,1024]{1,0:T(8,128)}, f32[72,1024]{1,0:T(8,128)S(1)}, u32[]{:S(2)}) copy-start(f32[72,1024]{1,0:T(8,128)S(1)} %collective-permute-done.before_ref) | copy-start | bytes 884740
  28.7 2.0 %copy-start.3 = (f32[72,1024]{1,0:T(8,128)}, f32[72,1024]{1,0:T(8,128)S(1)}, u32[]{:S(2)}) copy-start(f32[72,1024]{1,0:T(8,128)S(1)} %collective-permute-done.1.after_ref) | copy-start | bytes 884740
  30.8 67.7 %all-to-all-start.1 = ((f32[32,144,128]{2,1,0:T(8,128)}), f32[32,144,128]{2,1,0:T(8,128)S(1)}, u32[]{:S(2)}, u32[]{:S(2)}) async-start(f32[32,144,128]{2,1,0:T(8,128)} %top.1), calls=%async_computation.1 | async-start | bytes 4718592 | tf_op jit(solution)/shard_map/all_to_all | solution.py:510
  98.4 1.4 %copy-start = (f32[32,144,128]{2,1,0:T(8,128)}, f32[32,144,128]{2,1,0:T(8,128)S(1)}, u32[]{:S(2)}) copy-start(f32[32,144,128]{2,1,0:T(8,128)S(1)} %all-to-all-done.1.slots_hbm) | copy-start | bytes 7077892

commit v3 on v2

--- a/solution.py
+++ b/solution.py
@@ -35,6 +35,7 @@
 PART_L = HALO_L
 PARTS = [slice(HALO * i, HALO * (i + 1)) for i in range(PTS // HALO)]
 VMEM_BYTES = 60 * 1024 * 1024
+LESS_VMEM = 50 * 1024 * 1024
 
 vmem = pl.BlockSpec(memory_space=pltpu.VMEM)
 hbm = pl.BlockSpec(memory_space=pl.ANY)
@@ -185,6 +186,10 @@
 
     spread_all(local_in_ref, local_ref, 2 * LEAVES - 2)
     spread_path(place_ref[0], group_ref, path_in_ref, path_ref)
+    low, middle, high = (matrix(path_ref, i) for i in (0, 2, 4))
+    path = dot(
+        dot(high, matrix(path_ref, 3)), dot(middle, dot(matrix(path_ref, 1), low))
+    )
     nodes = coef_ref
     offset, count = 0, LEAVES
     while count > 1:
@@ -197,10 +202,7 @@
         for i, value in enumerate(values):
             level_ref[i] = value
         offset, count = offset + count, count // 2
-    value = level_ref[0]
-    for i in range(PATH):
-        value = dot(matrix(path_ref, i), value)
-    packed = fold(value)
+    packed = fold(dot(path, level_ref[0]))
     for g in range(GROUPS):
         roots_ref[g] = packed
     store(roots_ref, roots_hbm)
@@ -345,15 +347,14 @@
 
 
 def far_kernel(
-    recv_ref, slots_hbm, coupling_hbm, basis_hbm, wide_basis_hbm, near_hbm,
-    out_hbm, slots_ref, coupling_ref, basis_ref, wide_basis_ref, near_ref, turned_ref,
+    recv_ref, slots_ref, coupling_hbm, basis_hbm, wide_basis_hbm, near_hbm,
+    out_hbm, coupling_ref, basis_ref, wide_basis_ref, near_ref, turned_ref,
     sems, out_sems,
 ):
     loads = [
         pltpu.make_async_copy(source, target, sems.at[i])
         for i, (source, target) in enumerate(
             (
-                (slots_hbm, slots_ref),
                 (coupling_hbm, coupling_ref),
                 (basis_hbm, basis_ref),
                 (wide_basis_hbm, wide_basis_ref),
@@ -363,12 +364,11 @@
     ]
     for load in loads:
         load.start()
-    for load in loads[:2]:
-        load.wait()
     top = slots_ref[0, 4 * RANK :, :]
     for d in range(1, MEMBERS):
         top = top + slots_ref[d, 4 * RANK :, :]
     top = turned_parts(unfold(top))[:RHS]
+    loads[0].wait()
     left = left_half((RANK, 2 * RHS))
 
     def far(a):
@@ -392,7 +392,7 @@
         return carry
 
     lax.fori_loop(0, LEAVES // 2, turn, 0, unroll=8)
-    for load in loads[2:]:
+    for load in loads[1:]:
         load.wait()
 
     def finish(a, carry):
@@ -418,7 +418,7 @@
         copy.wait()
 
 
-def call(kernel, name, outs, specs, scratch, kind=f32, out=vmem, aliases=None):
+def call(kernel, name, outs, specs, scratch, kind=f32, out=vmem, aliases=None, limit=VMEM_BYTES):
     return pl.pallas_call(
         kernel,
         name=name,
@@ -427,7 +427,7 @@
         out_specs=[out] * len(outs),
         scratch_shapes=scratch,
         input_output_aliases=aliases or {},
-        compiler_params=pltpu.CompilerParams(vmem_limit_bytes=VMEM_BYTES),
+        compiler_params=pltpu.CompilerParams(vmem_limit_bytes=limit),
         cost_estimate=pl.CostEstimate(flops=10**9, bytes_accessed=2**20, transcendentals=0),
     )
 
@@ -518,6 +518,7 @@
             pltpu.VMEM((WIN, FEATURES), bf16),
             pltpu.VMEM((2 * RHS, WIN), bf16),
         ],
+        limit=LESS_VMEM,
     )(near_list, points, before, after)
 
     coupling, wide_basis = call(
@@ -527,23 +528,24 @@
         [smem] + [vmem] * 4,
         [pltpu.VMEM((LEAVES * INTER * RANK, LEAF), f32)] + wide,
         bf16,
+        limit=LESS_VMEM,
     )(place, leaf_coupling, local_transfer, group_transfer, leaf_basis)
     (potential,) = call(
         far_kernel,
         "far",
         [(RHS, PTS)],
-        [smem] + [hbm] * 5,
+        [smem, vmem] + [hbm] * 4,
         [
-            pltpu.VMEM((MEMBERS, 4 * RANK + RANK // 2, 2 * RHS), f32),
             pltpu.VMEM((LEAVES, 2 * RANK, INTER * RANK), bf16),
             pltpu.VMEM((RANK, PTS), f32),
             pltpu.VMEM((2 * RANK, PTS), bf16),
             pltpu.VMEM((RHS, PTS), f32),
             pltpu.VMEM((LEAVES // 2, 2 * RHS, 2 * RHS), bf16),
-            pltpu.SemaphoreType.DMA((5,)),
+            pltpu.SemaphoreType.DMA((4,)),
             pltpu.SemaphoreType.DMA((len(PARTS),)),
         ],
         out=hbm,
+        limit=LESS_VMEM,
     )(recv_list, slots, coupling, leaf_basis, wide_basis, near)
     return potential
 

time: 106 us -> 104 us (0.981)
  Pallas kernels: 63.8 us -> 58.9 us
  waiting for transfers between devices: 17.2 us -> 19.2 us
    pallas_call x1, Pallas kernels: 10.4 us -> 8.21 us  [shards(): call(weights_kernel, 'weights', [(LEAVES, 2 * RANK, INTER * RANK), (2 * R...]
    all_to_all x1, waiting for transfers between devices: 15.6 us -> 17.6 us  [shards(): slots = lax.all_to_all(sent, 'dev', split_axis=0, concat_axis=0, tiled=True)]
    pallas_call x1, Pallas kernels: 29.9 us -> 28.2 us  [shards(): call(near_kernel, 'near', [(RHS, PTS)], [smem, vmem, vmem, vmem], [pltpu....]
    unnamed x8 -> x20, local copies, waits for them, and re-layouts: 2.02 us -> 2.53 us
  transfers between devices with their start and end apart: 4 -> 4, of which waited for: 2 -> 2; matrix products, arithmetic and copies ran while one was open for 0% -> 0% of each run, Pallas kernels for 41% -> 38%
where the time goes in v3:
time: 104 us; the launch traced here: 103 us
  Pallas kernels  58.9 us (57%)
  starting transfers between devices  22.7 us (22%)
  waiting for transfers between devices  19.2 us (18%)
  local copies, waits for them, and re-layouts  2.53 us (2%)
    pallas_call x1, Pallas kernels, shards(): call(near_kernel, 'near', [(RHS, PTS)], [smem, vmem, vmem, vmem], [pltpu....  28.2 us
    all_to_all x1, waiting for transfers between devices, shards(): slots = lax.all_to_all(sent, 'dev', split_axis=0, concat_axis=0, tiled=True)  17.6 us
    pallas_call x1, Pallas kernels, shards(): call(order_kernel, 'order', [(RHS + 8, PTS), (RHS + 8, HALO), (RHS + 8, H...  12.2 us
    all_to_all x1, starting transfers between devices, shards(): slots = lax.all_to_all(sent, 'dev', split_axis=0, concat_axis=0, tiled=True)  11.9 us
    pallas_call x1, Pallas kernels, shards(): call(weights_kernel, 'weights', [(LEAVES, 2 * RANK, INTER * RANK), (2 * R...  8.21 us
    all_to_all x1, starting transfers between devices, shards(): lax.all_to_all(roots, 'group', split_axis=0, concat_axis=0, tiled=True)  5.54 us
    pallas_call x1, Pallas kernels, shards(): call(far_kernel, 'far', [(RHS, PTS)], [smem, vmem] + [hbm] * 4, [pltpu.VM...  5.09 us
    pallas_call x1, Pallas kernels, shards(): call(pack_kernel, 'pack', [(MEMBERS, 4 * RANK + RANK // 2, 2 * RHS)], [sm...  3.19 us
  transfers between devices with their start and end apart: 4, of which 2 were waited for; matrix products, arithmetic and copies ran while one was open for 0% of the time, Pallas kernels for 38%

profile of v3, /device:TPU:17, one launch (start us, length us, event | category | flops | bytes accessed | tf_op | source)
XLA Modules:
  0.0 103.5 jit_solution(18129987108477176049)
XLA Ops:
  0.0 12.2 %order.1 = (f32[72,4096]{1,0:T(8,128)}, f32[72,1024]{1,0:T(8,128)}, f32[72,1024]{1,0:T(8,128)}, f32[32,32,128]{2,1,0:T(8,128)}, f32[8,16,128]{2,1,0:T(8,128)}) custom-call(s32[1]{0:T(128)} %bitcast.place_ref, s32[1,4096]{1,0:T(1,128)} %order_ref.1, f32[64,4096]{1,0:T(8,128)} %charges_hbm.1, f32[3,4096]{1,0:T(4,128)} %coords_ref.1, f32[32,4096]{1,0:T(8,128)} %basis_hbm.3, ...), custom_call_target="tpu_custom_call" | custom-call | flops 1000000000 | bytes 1048576 | tf_op jit(solution)/shard_map/order/pallas_call | solution.py:454
  12.2 2.9 %collective-permute-start = (f32[72,1024]{1,0:T(8,128)}, f32[72,1024]{1,0:T(8,128)S(1)}, u32[]{:S(2)}, u32[]{:S(2)}) collective-permute-start(f32[72,1024]{1,0:T(8,128)} %get-tuple-element.16), channel_id=1, source_target_pairs={{0,1},{1,2},{2,3},{3,4},{4,5},{5,6},{6,7},{7,8},{8,9},{9,10},{10,1... | collective-permute-start | bytes 884744 | tf_op jit(solution)/shard_map/ppermute | solution.py:498
  15.1 2.4 %collective-permute-start.1 = (f32[72,1024]{1,0:T(8,128)}, f32[72,1024]{1,0:T(8,128)S(1)}, u32[]{:S(2)}, u32[]{:S(2)}) collective-permute-start(f32[72,1024]{1,0:T(8,128)} %get-tuple-element.17), channel_id=1, source_target_pairs={{1,0},{2,1},{3,2},{4,3},{5,4},{6,5},{7,6},{8,7},{9,8},{10,9},{11,1... | collective-permute-start | bytes 884744 | tf_op jit(solution)/shard_map/ppermute | solution.py:499
  17.5 5.5 %all-to-all-start = ((f32[8,16,128]{2,1,0:T(8,128)}), f32[8,16,128]{2,1,0:T(8,128)S(1)}, u32[]{:S(2)}, u32[]{:S(2)}) async-start(f32[8,16,128]{2,1,0:T(8,128)} %get-tuple-element.15), calls=%async_computation | async-start | bytes 131072 | tf_op jit(solution)/shard_map/all_to_all | solution.py:494
  23.0 3.2 %pack.1.sent_in_hbm = f32[32,144,128]{2,1,0:T(8,128)} custom-call(s32[1,256]{1,0:T(1,128)} %send_ref.1, f32[32,32,128]{2,1,0:T(8,128)} %get-tuple-element.19.coef_hbm), custom_call_target="tpu_custom_call" | custom-call | flops 1000000000 | bytes 1048576 | tf_op jit(solution)/shard_map/pack/pallas_call | solution.py:482
  26.2 1.7 %all-to-all-done.roots_ref = f32[8,16,128]{2,1,0:T(8,128)S(1)} async-done(((f32[8,16,128]{2,1,0:T(8,128)}), f32[8,16,128]{2,1,0:T(8,128)S(1)}, u32[]{:S(2)}, u32[]{:S(2)}) %all-to-all-start) | async-done | bytes 65568 | tf_op jit(solution)/shard_map/all_to_all | solution.py:494
  27.9 0.0 copy-start.9
  27.9 0.0 collective-permute-done.before_ref
  27.9 0.0 collective-permute-done.1.after_ref
  27.9 0.6 copy-done.9
  28.5 0.0 copy-start.3
  28.5 2.0 %top.1 = f32[32,144,128]{2,1,0:T(8,128)} custom-call(f32[8,16,128]{2,1,0:T(8,128)} %copy-done.9, f32[1,32,256]{2,1,0:T(8,128)} %top_ref.1, f32[32,144,128]{2,1,0:T(8,128)} %pack.1.sent_in_hbm), custom_call_target="tpu_custom_call", output_to_operand_aliasing={{}: (2, {})} | custom-call | flops 1000000000 | bytes 1048576 | tf_op jit(solution)/shard_map/top/pallas_call | solution.py:501
  30.5 0.0 copy-done.3
  30.5 0.0 copy-start
  30.5 0.0 copy-start.2
  30.5 11.9 %all-to-all-start.1 = ((f32[32,144,128]{2,1,0:T(8,128)}), f32[32,144,128]{2,1,0:T(8,128)}, u32[]{:S(2)}, u32[]{:S(2)}) async-start(f32[32,144,128]{2,1,0:T(8,128)} %top.1), calls=%async_computation.1 | async-start | bytes 4718592 | tf_op jit(solution)/shard_map/all_to_all | solution.py:510
  42.4 0.0 copy-done
  42.4 0.0 copy-done.2
  42.4 0.0 copy-start.5
  42.4 0.9 copy-done.5
  43.4 0.9 copy-done.6
  44.3 0.0 copy-start.4
  44.3 0.0 copy-start.7
  44.3 8.2 %weights.1 = (bf16[32,64,256]{2,1,0:T(8,128)(2,1)S(1)}, bf16[64,4096]{1,0:T(8,128)(2,1)S(1)}) custom-call(s32[1]{0:T(128)} %bitcast.place_ref, f32[256,1024]{1,0:T(8,128)S(1)} %copy-done.2, f32[62,1024]{1,0:T(8,128)S(1)} %copy-done.5, f32[62,1024]{1,0:T(8,128)S(1)} %copy-done.6, f32[32,4096]{1,0:T(8,128)S(1)} %copy-done), custom_call_target="tpu_custom_call" | custom-call | flops 1000000000 | bytes 1048576 | tf_op jit(solution)/shard_map/weights/pallas_call | solution.py:524
  52.6 0.0 copy-start.1
  52.6 0.0 copy-done.4
  52.6 0.0 copy-done.7
  52.6 0.0 copy-done.8
  52.6 28.2 %near.1.near_hbm = f32[64,4096]{1,0:T(8,128)S(1)} custom-call(s32[32,27]{1,0:T(8,128)S(1)} %copy-done.7, f32[72,4096]{1,0:T(8,128)S(1)} %copy-done.8, f32[72,1024]{1,0:T(8,128)S(1)} %collective-permute-done.before_ref, f32[72,1024]{1,0:T(8,128)S(1)} %copy-done.4), custom_call_target="tpu_custom_call" | custom-call | flops 1000000000 | bytes 1048576 | tf_op jit(solution)/shard_map/near/pallas_call | solution.py:511
  80.8 17.6 %all-to-all-done.1.slots_ref = f32[32,144,128]{2,1,0:T(8,128)} async-done(((f32[32,144,128]{2,1,0:T(8,128)}), f32[32,144,128]{2,1,0:T(8,128)}, u32[]{:S(2)}, u32[]{:S(2)}) %all-to-all-start.1) | async-done | bytes 2359328 | tf_op jit(solution)/shard_map/all_to_all | solution.py:510
  98.4 0.0 copy-done.1
  98.4 5.1 %far.1 = f32[64,4096]{1,0:T(8,128)} custom-call(s32[1,256]{1,0:T(1,128)S(1)} %copy-done.1, f32[32,144,128]{2,1,0:T(8,128)} %all-to-all-done.1.slots_ref, bf16[32,64,256]{2,1,0:T(8,128)(2,1)S(1)} %get-tuple-element.20.coupling_hbm, f32[32,4096]{1,0:T(8,128)S(1)} %copy-done, bf16[64,4096]{1,0:T(8,128)(2,1)S(1)} %get-tuple-element.21.wide_basis_hbm, ...), custom_call_target="tpu_custom_call" | custom-call | flops 1000000000 | bytes 1048576 | tf_op jit(solution)/shard_map/far/pallas_call | solution.py:533
  (2 shorter events, 0.0 us)
Async XLA Ops:
  12.2 15.7 %collective-permute-start = (f32[72,1024]{1,0:T(8,128)}, f32[72,1024]{1,0:T(8,128)S(1)}, u32[]{:S(2)}, u32[]{:S(2)}) collective-permute-start(f32[72,1024]{1,0:T(8,128)} %get-tuple-element.16), channel_id=1, source_target_pairs={{0,1},{1,2},{2,3},{3,4},{4,5},{5,6},{6,7},{7,8},{8,9},{9,10},{10,1... | collective-permute-start | bytes 884744 | tf_op jit(solution)/shard_map/ppermute | solution.py:498
  15.1 12.8 %collective-permute-start.1 = (f32[72,1024]{1,0:T(8,128)}, f32[72,1024]{1,0:T(8,128)S(1)}, u32[]{:S(2)}, u32[]{:S(2)}) collective-permute-start(f32[72,1024]{1,0:T(8,128)} %get-tuple-element.17), channel_id=1, source_target_pairs={{1,0},{2,1},{3,2},{4,3},{5,4},{6,5},{7,6},{8,7},{9,8},{10,9},{11,1... | collective-permute-start | bytes 884744 | tf_op jit(solution)/shard_map/ppermute | solution.py:499
  17.5 10.4 %all-to-all-start = ((f32[8,16,128]{2,1,0:T(8,128)}), f32[8,16,128]{2,1,0:T(8,128)S(1)}, u32[]{:S(2)}, u32[]{:S(2)}) async-start(f32[8,16,128]{2,1,0:T(8,128)} %get-tuple-element.15), calls=%async_computation | async-start | bytes 131072 | tf_op jit(solution)/shard_map/all_to_all | solution.py:494
  27.9 0.6 copy-start.9
  28.5 2.0 %copy-start.3 = (f32[72,1024]{1,0:T(8,128)}, f32[72,1024]{1,0:T(8,128)S(1)}, u32[]{:S(2)}) copy-start(f32[72,1024]{1,0:T(8,128)S(1)} %collective-permute-done.1.after_ref) | copy-start | bytes 884740
  30.5 11.9 %copy-start = (f32[32,4096]{1,0:T(8,128)S(1)}, f32[32,4096]{1,0:T(8,128)}, u32[]{:S(2)}) copy-start(f32[32,4096]{1,0:T(8,128)} %basis_hbm.3) | copy-start | bytes 1572868
  30.5 11.9 %copy-start.2 = (f32[256,1024]{1,0:T(8,128)S(1)}, f32[256,1024]{1,0:T(8,128)}, u32[]{:S(2)}) copy-start(f32[256,1024]{1,0:T(8,128)} %coupling_in_ref.1) | copy-start | bytes 3145732
  30.5 67.9 %all-to-all-start.1 = ((f32[32,144,128]{2,1,0:T(8,128)}), f32[32,144,128]{2,1,0:T(8,128)}, u32[]{:S(2)}, u32[]{:S(2)}) async-start(f32[32,144,128]{2,1,0:T(8,128)} %top.1), calls=%async_computation.1 | async-start | bytes 4718592 | tf_op jit(solution)/shard_map/all_to_all | solution.py:510
  42.4 1.0 copy-start.5
  43.4 0.9 copy-start.6
  44.3 8.2 %copy-start.4 = (f32[72,1024]{1,0:T(8,128)S(1)}, f32[72,1024]{1,0:T(8,128)}, u32[]{:S(2)}) copy-start(f32[72,1024]{1,0:T(8,128)} %copy-done.3) | copy-start | bytes 884740
  44.3 8.2 %copy-start.7 = (s32[32,27]{1,0:T(8,128)S(1)}, s32[32,27]{1,0:T(8,128)}, u32[]{:S(2)}) copy-start(s32[32,27]{1,0:T(8,128)} %list_ref.1) | copy-start | bytes 10372
  44.3 8.2 %copy-start.8 = (f32[72,4096]{1,0:T(8,128)S(1)}, f32[72,4096]{1,0:T(8,128)}, u32[]{:S(2)}) copy-start(f32[72,4096]{1,0:T(8,128)} %get-tuple-element.22.points_ref) | copy-start | bytes 3538948
  52.6 45.8 %copy-start.1 = (s32[1,256]{1,0:T(1,128)S(1)}, s32[1,256]{1,0:T(1,128)}, u32[]{:S(2)}) copy-start(s32[1,256]{1,0:T(1,128)} %recv_ref.1) | copy-start | bytes 3076

commit v4 on v3

--- a/solution.py
+++ b/solution.py
@@ -9,7 +9,7 @@
 
 f32 = jnp.float32
 bf16 = jnp.bfloat16
-highest = lax.Precision.HIGHEST
+precise = lax.Precision.HIGH
 
 LEAF = 128
 RANK = 32
@@ -47,7 +47,7 @@
 
 
 def dot(a, b):
-    return jnp.dot(a, b, precision=highest, preferred_element_type=f32)
+    return jnp.dot(a, b, precision=precise, preferred_element_type=f32)
 
 
 def left_half(shape):
@@ -140,7 +140,7 @@
 
     for i in range(len(PARTS)):
         loads[i].wait()
-        lax.fori_loop(PART_L * i, PART_L * (i + 1), turn, 0, unroll=4)
+        lax.fori_loop(PART_L * i, PART_L * (i + 1), turn, 0, unroll=8)
 
     def fetch(b, carry):
         for i in range(64):
@@ -175,7 +175,7 @@
         stores.append(copy)
 
     for i, part in enumerate(PARTS):
-        lax.fori_loop(PART_L * i, PART_L * (i + 1), coefficient, 0, unroll=4)
+        lax.fori_loop(PART_L * i, PART_L * (i + 1), coefficient, 0, unroll=8)
         leaves = slice(PART_L * i, PART_L * (i + 1))
         store(coef_ref.at[leaves], coef_hbm.at[leaves])
         store(points_ref.at[:, part], points_hbm.at[:, part])

time: 104 us -> 101 us (0.971)
  Pallas kernels: 58.9 us -> 55.1 us
    pallas_call x1, Pallas kernels: 12.2 us -> 9.38 us  [shards(): call(order_kernel, 'order', [(RHS + 8, PTS), (RHS + 8, HALO), (RHS + 8, H...]
where the time goes in v4:
time: 101 us
  Pallas kernels  55.1 us (55%)
  starting transfers between devices  22.7 us (22%)
  waiting for transfers between devices  20.2 us (20%)
  local copies, waits for them, and re-layouts  2.53 us (3%)
    pallas_call x1, Pallas kernels, shards(): call(near_kernel, 'near', [(RHS, PTS)], [smem, vmem, vmem, vmem], [pltpu....  28.2 us
    all_to_all x1, waiting for transfers between devices, shards(): slots = lax.all_to_all(sent, 'dev', split_axis=0, concat_axis=0, tiled=True)  18.5 us
    all_to_all x1, starting transfers between devices, shards(): slots = lax.all_to_all(sent, 'dev', split_axis=0, concat_axis=0, tiled=True)  11.9 us
    pallas_call x1, Pallas kernels, shards(): call(order_kernel, 'order', [(RHS + 8, PTS), (RHS + 8, HALO), (RHS + 8, H...  9.38 us
    pallas_call x1, Pallas kernels, shards(): call(weights_kernel, 'weights', [(LEAVES, 2 * RANK, INTER * RANK), (2 * R...  7.28 us
    all_to_all x1, starting transfers between devices, shards(): lax.all_to_all(roots, 'group', split_axis=0, concat_axis=0, tiled=True)  5.54 us
    pallas_call x1, Pallas kernels, shards(): call(far_kernel, 'far', [(RHS, PTS)], [smem, vmem] + [hbm] * 4, [pltpu.VM...  5.09 us
    pallas_call x1, Pallas kernels, shards(): call(pack_kernel, 'pack', [(MEMBERS, 4 * RANK + RANK // 2, 2 * RHS)], [sm...  3.19 us
  transfers between devices with their start and end apart: 4, of which 2 were waited for; matrix products, arithmetic and copies ran while one was open for 0% of the time, Pallas kernels for 38%

profile of v4, /device:TPU:17, one launch (start us, length us, event | category | flops | bytes accessed | tf_op | source)
XLA Modules:
  0.0 100.7 jit_solution(8587461140383323149)
XLA Ops:
  0.0 9.4 %order.1 = (f32[72,4096]{1,0:T(8,128)}, f32[72,1024]{1,0:T(8,128)}, f32[72,1024]{1,0:T(8,128)}, f32[32,32,128]{2,1,0:T(8,128)}, f32[8,16,128]{2,1,0:T(8,128)}) custom-call(s32[1]{0:T(128)} %bitcast.place_ref, s32[1,4096]{1,0:T(1,128)} %order_ref.1, f32[64,4096]{1,0:T(8,128)} %charges_hbm.1, f32[3,4096]{1,0:T(4,128)} %coords_ref.1, f32[32,4096]{1,0:T(8,128)} %basis_hbm.3, ...), custom_call_target="tpu_custom_call" | custom-call | flops 1000000000 | bytes 1048576 | tf_op jit(solution)/shard_map/order/pallas_call | solution.py:454
  9.4 2.9 %collective-permute-start = (f32[72,1024]{1,0:T(8,128)}, f32[72,1024]{1,0:T(8,128)S(1)}, u32[]{:S(2)}, u32[]{:S(2)}) collective-permute-start(f32[72,1024]{1,0:T(8,128)} %get-tuple-element.16), channel_id=1, source_target_pairs={{0,1},{1,2},{2,3},{3,4},{4,5},{5,6},{6,7},{7,8},{8,9},{9,10},{10,1... | collective-permute-start | bytes 884744 | tf_op jit(solution)/shard_map/ppermute | solution.py:498
  12.3 2.4 %collective-permute-start.1 = (f32[72,1024]{1,0:T(8,128)}, f32[72,1024]{1,0:T(8,128)S(1)}, u32[]{:S(2)}, u32[]{:S(2)}) collective-permute-start(f32[72,1024]{1,0:T(8,128)} %get-tuple-element.17), channel_id=1, source_target_pairs={{1,0},{2,1},{3,2},{4,3},{5,4},{6,5},{7,6},{8,7},{9,8},{10,9},{11,1... | collective-permute-start | bytes 884744 | tf_op jit(solution)/shard_map/ppermute | solution.py:499
  14.7 5.5 %all-to-all-start = ((f32[8,16,128]{2,1,0:T(8,128)}), f32[8,16,128]{2,1,0:T(8,128)S(1)}, u32[]{:S(2)}, u32[]{:S(2)}) async-start(f32[8,16,128]{2,1,0:T(8,128)} %get-tuple-element.15), calls=%async_computation | async-start | bytes 131072 | tf_op jit(solution)/shard_map/all_to_all | solution.py:494
  20.2 3.2 %pack.1.sent_in_hbm = f32[32,144,128]{2,1,0:T(8,128)} custom-call(s32[1,256]{1,0:T(1,128)} %send_ref.1, f32[32,32,128]{2,1,0:T(8,128)} %get-tuple-element.19.coef_hbm), custom_call_target="tpu_custom_call" | custom-call | flops 1000000000 | bytes 1048576 | tf_op jit(solution)/shard_map/pack/pallas_call | solution.py:482
  23.4 1.7 %all-to-all-done.roots_ref = f32[8,16,128]{2,1,0:T(8,128)S(1)} async-done(((f32[8,16,128]{2,1,0:T(8,128)}), f32[8,16,128]{2,1,0:T(8,128)S(1)}, u32[]{:S(2)}, u32[]{:S(2)}) %all-to-all-start) | async-done | bytes 65568 | tf_op jit(solution)/shard_map/all_to_all | solution.py:494
  25.1 0.0 copy-start.9
  25.1 0.0 collective-permute-done.before_ref
  25.1 0.0 collective-permute-done.1.after_ref
  25.1 0.6 copy-done.9
  25.7 0.0 copy-start.3
  25.7 1.9 %top.1 = f32[32,144,128]{2,1,0:T(8,128)} custom-call(f32[8,16,128]{2,1,0:T(8,128)} %copy-done.9, f32[1,32,256]{2,1,0:T(8,128)} %top_ref.1, f32[32,144,128]{2,1,0:T(8,128)} %pack.1.sent_in_hbm), custom_call_target="tpu_custom_call", output_to_operand_aliasing={{}: (2, {})} | custom-call | flops 1000000000 | bytes 1048576 | tf_op jit(solution)/shard_map/top/pallas_call | solution.py:501
  27.7 0.0 copy-done.3
  27.7 0.0 copy-start
  27.7 0.0 copy-start.2
  27.7 11.9 %all-to-all-start.1 = ((f32[32,144,128]{2,1,0:T(8,128)}), f32[32,144,128]{2,1,0:T(8,128)}, u32[]{:S(2)}, u32[]{:S(2)}) async-start(f32[32,144,128]{2,1,0:T(8,128)} %top.1), calls=%async_computation.1 | async-start | bytes 4718592 | tf_op jit(solution)/shard_map/all_to_all | solution.py:510
  39.6 0.0 copy-done
  39.6 0.0 copy-done.2
  39.6 0.0 copy-start.5
  39.6 0.9 copy-done.5
  40.6 0.0 copy-start.6
  40.6 0.9 copy-done.6
  41.5 0.0 copy-start.7
  41.5 7.3 %weights.1 = (bf16[32,64,256]{2,1,0:T(8,128)(2,1)S(1)}, bf16[64,4096]{1,0:T(8,128)(2,1)S(1)}) custom-call(s32[1]{0:T(128)} %bitcast.place_ref, f32[256,1024]{1,0:T(8,128)S(1)} %copy-done.2, f32[62,1024]{1,0:T(8,128)S(1)} %copy-done.5, f32[62,1024]{1,0:T(8,128)S(1)} %copy-done.6, f32[32,4096]{1,0:T(8,128)S(1)} %copy-done), custom_call_target="tpu_custom_call" | custom-call | flops 1000000000 | bytes 1048576 | tf_op jit(solution)/shard_map/weights/pallas_call | solution.py:524
  48.8 0.0 copy-start.1
  48.8 0.0 copy-done.4
  48.8 0.0 copy-done.7
  48.8 0.0 copy-done.8
  48.9 28.2 %near.1.near_hbm = f32[64,4096]{1,0:T(8,128)S(1)} custom-call(s32[32,27]{1,0:T(8,128)S(1)} %copy-done.7, f32[72,4096]{1,0:T(8,128)S(1)} %copy-done.8, f32[72,1024]{1,0:T(8,128)S(1)} %collective-permute-done.before_ref, f32[72,1024]{1,0:T(8,128)S(1)} %copy-done.4), custom_call_target="tpu_custom_call" | custom-call | flops 1000000000 | bytes 1048576 | tf_op jit(solution)/shard_map/near/pallas_call | solution.py:511
  77.1 18.5 %all-to-all-done.1.slots_ref = f32[32,144,128]{2,1,0:T(8,128)} async-done(((f32[32,144,128]{2,1,0:T(8,128)}), f32[32,144,128]{2,1,0:T(8,128)}, u32[]{:S(2)}, u32[]{:S(2)}) %all-to-all-start.1) | async-done | bytes 2359328 | tf_op jit(solution)/shard_map/all_to_all | solution.py:510
  95.6 0.0 copy-done.1
  95.6 5.1 %far.1 = f32[64,4096]{1,0:T(8,128)} custom-call(s32[1,256]{1,0:T(1,128)S(1)} %copy-done.1, f32[32,144,128]{2,1,0:T(8,128)} %all-to-all-done.1.slots_ref, bf16[32,64,256]{2,1,0:T(8,128)(2,1)S(1)} %get-tuple-element.20.coupling_hbm, f32[32,4096]{1,0:T(8,128)S(1)} %copy-done, bf16[64,4096]{1,0:T(8,128)(2,1)S(1)} %get-tuple-element.21.wide_basis_hbm, ...), custom_call_target="tpu_custom_call" | custom-call | flops 1000000000 | bytes 1048576 | tf_op jit(solution)/shard_map/far/pallas_call | solution.py:533
  (2 shorter events, 0.0 us)
Async XLA Ops:
  9.4 15.7 %collective-permute-start = (f32[72,1024]{1,0:T(8,128)}, f32[72,1024]{1,0:T(8,128)S(1)}, u32[]{:S(2)}, u32[]{:S(2)}) collective-permute-start(f32[72,1024]{1,0:T(8,128)} %get-tuple-element.16), channel_id=1, source_target_pairs={{0,1},{1,2},{2,3},{3,4},{4,5},{5,6},{6,7},{7,8},{8,9},{9,10},{10,1... | collective-permute-start | bytes 884744 | tf_op jit(solution)/shard_map/ppermute | solution.py:498
  12.3 12.8 %collective-permute-start.1 = (f32[72,1024]{1,0:T(8,128)}, f32[72,1024]{1,0:T(8,128)S(1)}, u32[]{:S(2)}, u32[]{:S(2)}) collective-permute-start(f32[72,1024]{1,0:T(8,128)} %get-tuple-element.17), channel_id=1, source_target_pairs={{1,0},{2,1},{3,2},{4,3},{5,4},{6,5},{7,6},{8,7},{9,8},{10,9},{11,1... | collective-permute-start | bytes 884744 | tf_op jit(solution)/shard_map/ppermute | solution.py:499
  14.7 10.4 %all-to-all-start = ((f32[8,16,128]{2,1,0:T(8,128)}), f32[8,16,128]{2,1,0:T(8,128)S(1)}, u32[]{:S(2)}, u32[]{:S(2)}) async-start(f32[8,16,128]{2,1,0:T(8,128)} %get-tuple-element.15), calls=%async_computation | async-start | bytes 131072 | tf_op jit(solution)/shard_map/all_to_all | solution.py:494
  25.1 0.6 copy-start.9
  25.7 2.0 %copy-start.3 = (f32[72,1024]{1,0:T(8,128)}, f32[72,1024]{1,0:T(8,128)S(1)}, u32[]{:S(2)}) copy-start(f32[72,1024]{1,0:T(8,128)S(1)} %collective-permute-done.1.after_ref) | copy-start | bytes 884740
  27.7 11.9 %copy-start = (f32[32,4096]{1,0:T(8,128)S(1)}, f32[32,4096]{1,0:T(8,128)}, u32[]{:S(2)}) copy-start(f32[32,4096]{1,0:T(8,128)} %basis_hbm.3) | copy-start | bytes 1572868
  27.7 11.9 %copy-start.2 = (f32[256,1024]{1,0:T(8,128)S(1)}, f32[256,1024]{1,0:T(8,128)}, u32[]{:S(2)}) copy-start(f32[256,1024]{1,0:T(8,128)} %coupling_in_ref.1) | copy-start | bytes 3145732
  27.7 67.9 %all-to-all-start.1 = ((f32[32,144,128]{2,1,0:T(8,128)}), f32[32,144,128]{2,1,0:T(8,128)}, u32[]{:S(2)}, u32[]{:S(2)}) async-start(f32[32,144,128]{2,1,0:T(8,128)} %top.1), calls=%async_computation.1 | async-start | bytes 4718592 | tf_op jit(solution)/shard_map/all_to_all | solution.py:510
  39.6 1.0 copy-start.5
  40.6 0.9 copy-start.6
  41.5 7.3 %copy-start.4 = (f32[72,1024]{1,0:T(8,128)S(1)}, f32[72,1024]{1,0:T(8,128)}, u32[]{:S(2)}) copy-start(f32[72,1024]{1,0:T(8,128)} %copy-done.3) | copy-start | bytes 884740
  41.5 7.3 %copy-start.7 = (s32[32,27]{1,0:T(8,128)S(1)}, s32[32,27]{1,0:T(8,128)}, u32[]{:S(2)}) copy-start(s32[32,27]{1,0:T(8,128)} %list_ref.1) | copy-start | bytes 10372
  41.5 7.3 %copy-start.8 = (f32[72,4096]{1,0:T(8,128)S(1)}, f32[72,4096]{1,0:T(8,128)}, u32[]{:S(2)}) copy-start(f32[72,4096]{1,0:T(8,128)} %get-tuple-element.22.points_ref) | copy-start | bytes 3538948
  48.8 46.8 %copy-start.1 = (s32[1,256]{1,0:T(1,128)S(1)}, s32[1,256]{1,0:T(1,128)}, u32[]{:S(2)}) copy-start(s32[1,256]{1,0:T(1,128)} %recv_ref.1) | copy-start | bytes 3076

commit v5 on v4

--- a/solution.py
+++ b/solution.py
@@ -9,7 +9,7 @@
 
 f32 = jnp.float32
 bf16 = jnp.bfloat16
-precise = lax.Precision.HIGH
+precise = lax.Precision.HIGHEST
 
 LEAF = 128
 RANK = 32

time: 101 us -> 102 us (level)
  Pallas kernels: 55.1 us -> 56.8 us
  transfers between devices with their start and end apart: 4 -> 4, of which waited for: 2 -> 2; matrix products, arithmetic and copies ran while one was open for 0% -> 0% of each run, Pallas kernels for 38% -> 39%
where the time goes in v5:
time: 102 us; the launch traced here: 101 us
  Pallas kernels  56.8 us (56%)
  starting transfers between devices  22.7 us (22%)
  waiting for transfers between devices  19.2 us (19%)
  local copies, waits for them, and re-layouts  2.53 us (2%)
    pallas_call x1, Pallas kernels, shards(): call(near_kernel, 'near', [(RHS, PTS)], [smem, vmem, vmem, vmem], [pltpu....  28.2 us
    all_to_all x1, waiting for transfers between devices, shards(): slots = lax.all_to_all(sent, 'dev', split_axis=0, concat_axis=0, tiled=True)  17.6 us
    all_to_all x1, starting transfers between devices, shards(): slots = lax.all_to_all(sent, 'dev', split_axis=0, concat_axis=0, tiled=True)  11.9 us
    pallas_call x1, Pallas kernels, shards(): call(order_kernel, 'order', [(RHS + 8, PTS), (RHS + 8, HALO), (RHS + 8, H...  10.1 us
    pallas_call x1, Pallas kernels, shards(): call(weights_kernel, 'weights', [(LEAVES, 2 * RANK, INTER * RANK), (2 * R...  8.21 us
    all_to_all x1, starting transfers between devices, shards(): lax.all_to_all(roots, 'group', split_axis=0, concat_axis=0, tiled=True)  5.55 us
    pallas_call x1, Pallas kernels, shards(): call(far_kernel, 'far', [(RHS, PTS)], [smem, vmem] + [hbm] * 4, [pltpu.VM...  5.09 us
    pallas_call x1, Pallas kernels, shards(): call(pack_kernel, 'pack', [(MEMBERS, 4 * RANK + RANK // 2, 2 * RHS)], [sm...  3.19 us
  transfers between devices with their start and end apart: 4, of which 2 were waited for; matrix products, arithmetic and copies ran while one was open for 0% of the time, Pallas kernels for 39%

profile of v5, /device:TPU:17, one launch (start us, length us, event | category | flops | bytes accessed | tf_op | source)
XLA Modules:
  0.0 101.4 jit_solution(16638452375244409733)
XLA Ops:
  0.0 10.1 %order.1 = (f32[72,4096]{1,0:T(8,128)}, f32[72,1024]{1,0:T(8,128)}, f32[72,1024]{1,0:T(8,128)}, f32[32,32,128]{2,1,0:T(8,128)}, f32[8,16,128]{2,1,0:T(8,128)}) custom-call(s32[1]{0:T(128)} %bitcast.place_ref, s32[1,4096]{1,0:T(1,128)} %order_ref.1, f32[64,4096]{1,0:T(8,128)} %charges_hbm.1, f32[3,4096]{1,0:T(4,128)} %coords_ref.1, f32[32,4096]{1,0:T(8,128)} %basis_hbm.3, ...), custom_call_target="tpu_custom_call" | custom-call | flops 1000000000 | bytes 1048576 | tf_op jit(solution)/shard_map/order/pallas_call | solution.py:454
  10.1 2.9 %collective-permute-start = (f32[72,1024]{1,0:T(8,128)}, f32[72,1024]{1,0:T(8,128)S(1)}, u32[]{:S(2)}, u32[]{:S(2)}) collective-permute-start(f32[72,1024]{1,0:T(8,128)} %get-tuple-element.16), channel_id=1, source_target_pairs={{0,1},{1,2},{2,3},{3,4},{4,5},{5,6},{6,7},{7,8},{8,9},{9,10},{10,1... | collective-permute-start | bytes 884744 | tf_op jit(solution)/shard_map/ppermute | solution.py:498
  13.0 2.4 %collective-permute-start.1 = (f32[72,1024]{1,0:T(8,128)}, f32[72,1024]{1,0:T(8,128)S(1)}, u32[]{:S(2)}, u32[]{:S(2)}) collective-permute-start(f32[72,1024]{1,0:T(8,128)} %get-tuple-element.17), channel_id=1, source_target_pairs={{1,0},{2,1},{3,2},{4,3},{5,4},{6,5},{7,6},{8,7},{9,8},{10,9},{11,1... | collective-permute-start | bytes 884744 | tf_op jit(solution)/shard_map/ppermute | solution.py:499
  15.4 5.5 %all-to-all-start = ((f32[8,16,128]{2,1,0:T(8,128)}), f32[8,16,128]{2,1,0:T(8,128)S(1)}, u32[]{:S(2)}, u32[]{:S(2)}) async-start(f32[8,16,128]{2,1,0:T(8,128)} %get-tuple-element.15), calls=%async_computation | async-start | bytes 131072 | tf_op jit(solution)/shard_map/all_to_all | solution.py:494
  21.0 3.2 %pack.1.sent_in_hbm = f32[32,144,128]{2,1,0:T(8,128)} custom-call(s32[1,256]{1,0:T(1,128)} %send_ref.1, f32[32,32,128]{2,1,0:T(8,128)} %get-tuple-element.19.coef_hbm), custom_call_target="tpu_custom_call" | custom-call | flops 1000000000 | bytes 1048576 | tf_op jit(solution)/shard_map/pack/pallas_call | solution.py:482
  24.1 1.7 %all-to-all-done.roots_ref = f32[8,16,128]{2,1,0:T(8,128)S(1)} async-done(((f32[8,16,128]{2,1,0:T(8,128)}), f32[8,16,128]{2,1,0:T(8,128)S(1)}, u32[]{:S(2)}, u32[]{:S(2)}) %all-to-all-start) | async-done | bytes 65568 | tf_op jit(solution)/shard_map/all_to_all | solution.py:494
  25.8 0.0 copy-start.9
  25.8 0.0 collective-permute-done.before_ref
  25.8 0.0 collective-permute-done.1.after_ref
  25.8 0.6 copy-done.9
  26.4 0.0 copy-start.3
  26.4 2.0 %top.1 = f32[32,144,128]{2,1,0:T(8,128)} custom-call(f32[8,16,128]{2,1,0:T(8,128)} %copy-done.9, f32[1,32,256]{2,1,0:T(8,128)} %top_ref.1, f32[32,144,128]{2,1,0:T(8,128)} %pack.1.sent_in_hbm), custom_call_target="tpu_custom_call", output_to_operand_aliasing={{}: (2, {})} | custom-call | flops 1000000000 | bytes 1048576 | tf_op jit(solution)/shard_map/top/pallas_call | solution.py:501
  28.4 0.0 copy-done.3
  28.4 0.0 copy-start
  28.4 0.0 copy-start.2
  28.4 11.9 %all-to-all-start.1 = ((f32[32,144,128]{2,1,0:T(8,128)}), f32[32,144,128]{2,1,0:T(8,128)}, u32[]{:S(2)}, u32[]{:S(2)}) async-start(f32[32,144,128]{2,1,0:T(8,128)} %top.1), calls=%async_computation.1 | async-start | bytes 4718592 | tf_op jit(solution)/shard_map/all_to_all | solution.py:510
  40.3 0.0 copy-done
  40.4 0.0 copy-done.2
  40.4 0.0 copy-start.5
  40.4 0.9 copy-done.5
  41.3 0.0 copy-start.6
  41.3 0.9 copy-done.6
  42.3 0.0 copy-start.4
  42.3 8.2 %weights.1 = (bf16[32,64,256]{2,1,0:T(8,128)(2,1)S(1)}, bf16[64,4096]{1,0:T(8,128)(2,1)S(1)}) custom-call(s32[1]{0:T(128)} %bitcast.place_ref, f32[256,1024]{1,0:T(8,128)S(1)} %copy-done.2, f32[62,1024]{1,0:T(8,128)S(1)} %copy-done.5, f32[62,1024]{1,0:T(8,128)S(1)} %copy-done.6, f32[32,4096]{1,0:T(8,128)S(1)} %copy-done), custom_call_target="tpu_custom_call" | custom-call | flops 1000000000 | bytes 1048576 | tf_op jit(solution)/shard_map/weights/pallas_call | solution.py:524
  50.5 0.0 copy-start.1
  50.5 0.0 copy-done.4
  50.5 0.0 copy-done.7
  50.5 0.0 copy-done.8
  50.5 28.2 %near.1.near_hbm = f32[64,4096]{1,0:T(8,128)S(1)} custom-call(s32[32,27]{1,0:T(8,128)S(1)} %copy-done.7, f32[72,4096]{1,0:T(8,128)S(1)} %copy-done.8, f32[72,1024]{1,0:T(8,128)S(1)} %collective-permute-done.before_ref, f32[72,1024]{1,0:T(8,128)S(1)} %copy-done.4), custom_call_target="tpu_custom_call" | custom-call | flops 1000000000 | bytes 1048576 | tf_op jit(solution)/shard_map/near/pallas_call | solution.py:511
  78.8 17.6 %all-to-all-done.1.slots_ref = f32[32,144,128]{2,1,0:T(8,128)} async-done(((f32[32,144,128]{2,1,0:T(8,128)}), f32[32,144,128]{2,1,0:T(8,128)}, u32[]{:S(2)}, u32[]{:S(2)}) %all-to-all-start.1) | async-done | bytes 2359328 | tf_op jit(solution)/shard_map/all_to_all | solution.py:510
  96.3 0.0 copy-done.1
  96.3 5.1 %far.1 = f32[64,4096]{1,0:T(8,128)} custom-call(s32[1,256]{1,0:T(1,128)S(1)} %copy-done.1, f32[32,144,128]{2,1,0:T(8,128)} %all-to-all-done.1.slots_ref, bf16[32,64,256]{2,1,0:T(8,128)(2,1)S(1)} %get-tuple-element.20.coupling_hbm, f32[32,4096]{1,0:T(8,128)S(1)} %copy-done, bf16[64,4096]{1,0:T(8,128)(2,1)S(1)} %get-tuple-element.21.wide_basis_hbm, ...), custom_call_target="tpu_custom_call" | custom-call | flops 1000000000 | bytes 1048576 | tf_op jit(solution)/shard_map/far/pallas_call | solution.py:533
  (2 shorter events, 0.0 us)
Async XLA Ops:
  10.1 15.7 %collective-permute-start = (f32[72,1024]{1,0:T(8,128)}, f32[72,1024]{1,0:T(8,128)S(1)}, u32[]{:S(2)}, u32[]{:S(2)}) collective-permute-start(f32[72,1024]{1,0:T(8,128)} %get-tuple-element.16), channel_id=1, source_target_pairs={{0,1},{1,2},{2,3},{3,4},{4,5},{5,6},{6,7},{7,8},{8,9},{9,10},{10,1... | collective-permute-start | bytes 884744 | tf_op jit(solution)/shard_map/ppermute | solution.py:498
  13.0 12.8 %collective-permute-start.1 = (f32[72,1024]{1,0:T(8,128)}, f32[72,1024]{1,0:T(8,128)S(1)}, u32[]{:S(2)}, u32[]{:S(2)}) collective-permute-start(f32[72,1024]{1,0:T(8,128)} %get-tuple-element.17), channel_id=1, source_target_pairs={{1,0},{2,1},{3,2},{4,3},{5,4},{6,5},{7,6},{8,7},{9,8},{10,9},{11,1... | collective-permute-start | bytes 884744 | tf_op jit(solution)/shard_map/ppermute | solution.py:499
  15.4 10.4 %all-to-all-start = ((f32[8,16,128]{2,1,0:T(8,128)}), f32[8,16,128]{2,1,0:T(8,128)S(1)}, u32[]{:S(2)}, u32[]{:S(2)}) async-start(f32[8,16,128]{2,1,0:T(8,128)} %get-tuple-element.15), calls=%async_computation | async-start | bytes 131072 | tf_op jit(solution)/shard_map/all_to_all | solution.py:494
  25.8 0.6 copy-start.9
  26.4 2.0 %copy-start.3 = (f32[72,1024]{1,0:T(8,128)}, f32[72,1024]{1,0:T(8,128)S(1)}, u32[]{:S(2)}) copy-start(f32[72,1024]{1,0:T(8,128)S(1)} %collective-permute-done.1.after_ref) | copy-start | bytes 884740
  28.4 11.9 %copy-start = (f32[32,4096]{1,0:T(8,128)S(1)}, f32[32,4096]{1,0:T(8,128)}, u32[]{:S(2)}) copy-start(f32[32,4096]{1,0:T(8,128)} %basis_hbm.3) | copy-start | bytes 1572868
  28.4 11.9 %copy-start.2 = (f32[256,1024]{1,0:T(8,128)S(1)}, f32[256,1024]{1,0:T(8,128)}, u32[]{:S(2)}) copy-start(f32[256,1024]{1,0:T(8,128)} %coupling_in_ref.1) | copy-start | bytes 3145732
  28.4 67.9 %all-to-all-start.1 = ((f32[32,144,128]{2,1,0:T(8,128)}), f32[32,144,128]{2,1,0:T(8,128)}, u32[]{:S(2)}, u32[]{:S(2)}) async-start(f32[32,144,128]{2,1,0:T(8,128)} %top.1), calls=%async_computation.1 | async-start | bytes 4718592 | tf_op jit(solution)/shard_map/all_to_all | solution.py:510
  40.4 1.0 copy-start.5
  41.3 0.9 copy-start.6
  42.3 8.2 %copy-start.4 = (f32[72,1024]{1,0:T(8,128)S(1)}, f32[72,1024]{1,0:T(8,128)}, u32[]{:S(2)}) copy-start(f32[72,1024]{1,0:T(8,128)} %copy-done.3) | copy-start | bytes 884740
  42.3 8.2 %copy-start.7 = (s32[32,27]{1,0:T(8,128)S(1)}, s32[32,27]{1,0:T(8,128)}, u32[]{:S(2)}) copy-start(s32[32,27]{1,0:T(8,128)} %list_ref.1) | copy-start | bytes 10372
  42.3 8.2 %copy-start.8 = (f32[72,4096]{1,0:T(8,128)S(1)}, f32[72,4096]{1,0:T(8,128)}, u32[]{:S(2)}) copy-start(f32[72,4096]{1,0:T(8,128)} %get-tuple-element.22.points_ref) | copy-start | bytes 3538948
  50.5 45.8 %copy-start.1 = (s32[1,256]{1,0:T(1,128)S(1)}, s32[1,256]{1,0:T(1,128)}, u32[]{:S(2)}) copy-start(s32[1,256]{1,0:T(1,128)} %recv_ref.1) | copy-start | bytes 3076

commit v6 on v5

--- a/solution.py
+++ b/solution.py
@@ -143,12 +143,12 @@
         lax.fori_loop(PART_L * i, PART_L * (i + 1), turn, 0, unroll=8)
 
     def fetch(b, carry):
-        for i in range(64):
-            at = b * 64 + i
+        for i in range(128):
+            at = b * 128 + i
             rows_ref[pl.ds(at, 1), :] = turned_ref[pl.ds(order_ref[0, at], 1), :]
         return carry
 
-    lax.fori_loop(0, PTS // 64, fetch, 0)
+    lax.fori_loop(0, PTS // 128, fetch, 0)
 
     def coefficient(l, carry):
         columns = block(l, LEAF)

time: 102 us -> 102 us (level)
  no operation moved by 1% of the time
where the time goes in v6:
time: 102 us; the launch traced here: 101 us
  Pallas kernels  56.7 us (56%)
  starting transfers between devices  22.7 us (22%)
  waiting for transfers between devices  19.2 us (19%)
  local copies, waits for them, and re-layouts  2.53 us (2%)
    pallas_call x1, Pallas kernels, shards(): call(near_kernel, 'near', [(RHS, PTS)], [smem, vmem, vmem, vmem], [pltpu....  28.3 us
    all_to_all x1, waiting for transfers between devices, shards(): slots = lax.all_to_all(sent, 'dev', split_axis=0, concat_axis=0, tiled=True)  17.5 us
    all_to_all x1, starting transfers between devices, shards(): slots = lax.all_to_all(sent, 'dev', split_axis=0, concat_axis=0, tiled=True)  11.9 us
    pallas_call x1, Pallas kernels, shards(): call(order_kernel, 'order', [(RHS + 8, PTS), (RHS + 8, HALO), (RHS + 8, H...  9.96 us
    pallas_call x1, Pallas kernels, shards(): call(weights_kernel, 'weights', [(LEAVES, 2 * RANK, INTER * RANK), (2 * R...  8.21 us
    all_to_all x1, starting transfers between devices, shards(): lax.all_to_all(roots, 'group', split_axis=0, concat_axis=0, tiled=True)  5.55 us
    pallas_call x1, Pallas kernels, shards(): call(far_kernel, 'far', [(RHS, PTS)], [smem, vmem] + [hbm] * 4, [pltpu.VM...  5.09 us
    pallas_call x1, Pallas kernels, shards(): call(pack_kernel, 'pack', [(MEMBERS, 4 * RANK + RANK // 2, 2 * RHS)], [sm...  3.19 us
  transfers between devices with their start and end apart: 4, of which 2 were waited for; matrix products, arithmetic and copies ran while one was open for 0% of the time, Pallas kernels for 39%

profile of v6, /device:TPU:17, one launch (start us, length us, event | category | flops | bytes accessed | tf_op | source)
XLA Modules:
  0.0 101.3 jit_solution(7313580879264680173)
XLA Ops:
  0.0 10.0 %order.1 = (f32[72,4096]{1,0:T(8,128)}, f32[72,1024]{1,0:T(8,128)}, f32[72,1024]{1,0:T(8,128)}, f32[32,32,128]{2,1,0:T(8,128)}, f32[8,16,128]{2,1,0:T(8,128)}) custom-call(s32[1]{0:T(128)} %bitcast.place_ref, s32[1,4096]{1,0:T(1,128)} %order_ref.1, f32[64,4096]{1,0:T(8,128)} %charges_hbm.1, f32[3,4096]{1,0:T(4,128)} %coords_ref.1, f32[32,4096]{1,0:T(8,128)} %basis_hbm.3, ...), custom_call_target="tpu_custom_call" | custom-call | flops 1000000000 | bytes 1048576 | tf_op jit(solution)/shard_map/order/pallas_call | solution.py:454
  10.0 2.9 %collective-permute-start = (f32[72,1024]{1,0:T(8,128)}, f32[72,1024]{1,0:T(8,128)S(1)}, u32[]{:S(2)}, u32[]{:S(2)}) collective-permute-start(f32[72,1024]{1,0:T(8,128)} %get-tuple-element.16), channel_id=1, source_target_pairs={{0,1},{1,2},{2,3},{3,4},{4,5},{5,6},{6,7},{7,8},{8,9},{9,10},{10,1... | collective-permute-start | bytes 884744 | tf_op jit(solution)/shard_map/ppermute | solution.py:498
  12.9 2.4 %collective-permute-start.1 = (f32[72,1024]{1,0:T(8,128)}, f32[72,1024]{1,0:T(8,128)S(1)}, u32[]{:S(2)}, u32[]{:S(2)}) collective-permute-start(f32[72,1024]{1,0:T(8,128)} %get-tuple-element.17), channel_id=1, source_target_pairs={{1,0},{2,1},{3,2},{4,3},{5,4},{6,5},{7,6},{8,7},{9,8},{10,9},{11,1... | collective-permute-start | bytes 884744 | tf_op jit(solution)/shard_map/ppermute | solution.py:499
  15.3 5.5 %all-to-all-start = ((f32[8,16,128]{2,1,0:T(8,128)}), f32[8,16,128]{2,1,0:T(8,128)S(1)}, u32[]{:S(2)}, u32[]{:S(2)}) async-start(f32[8,16,128]{2,1,0:T(8,128)} %get-tuple-element.15), calls=%async_computation | async-start | bytes 131072 | tf_op jit(solution)/shard_map/all_to_all | solution.py:494
  20.8 3.2 %pack.1.sent_in_hbm = f32[32,144,128]{2,1,0:T(8,128)} custom-call(s32[1,256]{1,0:T(1,128)} %send_ref.1, f32[32,32,128]{2,1,0:T(8,128)} %get-tuple-element.19.coef_hbm), custom_call_target="tpu_custom_call" | custom-call | flops 1000000000 | bytes 1048576 | tf_op jit(solution)/shard_map/pack/pallas_call | solution.py:482
  24.0 1.7 %all-to-all-done.roots_ref = f32[8,16,128]{2,1,0:T(8,128)S(1)} async-done(((f32[8,16,128]{2,1,0:T(8,128)}), f32[8,16,128]{2,1,0:T(8,128)S(1)}, u32[]{:S(2)}, u32[]{:S(2)}) %all-to-all-start) | async-done | bytes 65568 | tf_op jit(solution)/shard_map/all_to_all | solution.py:494
  25.7 0.0 copy-start.9
  25.7 0.0 collective-permute-done.before_ref
  25.7 0.0 collective-permute-done.1.after_ref
  25.7 0.6 copy-done.9
  26.3 0.0 copy-start.3
  26.3 2.0 %top.1 = f32[32,144,128]{2,1,0:T(8,128)} custom-call(f32[8,16,128]{2,1,0:T(8,128)} %copy-done.9, f32[1,32,256]{2,1,0:T(8,128)} %top_ref.1, f32[32,144,128]{2,1,0:T(8,128)} %pack.1.sent_in_hbm), custom_call_target="tpu_custom_call", output_to_operand_aliasing={{}: (2, {})} | custom-call | flops 1000000000 | bytes 1048576 | tf_op jit(solution)/shard_map/top/pallas_call | solution.py:501
  28.3 0.0 copy-done.3
  28.3 0.0 copy-start
  28.3 0.0 copy-start.2
  28.3 11.9 %all-to-all-start.1 = ((f32[32,144,128]{2,1,0:T(8,128)}), f32[32,144,128]{2,1,0:T(8,128)}, u32[]{:S(2)}, u32[]{:S(2)}) async-start(f32[32,144,128]{2,1,0:T(8,128)} %top.1), calls=%async_computation.1 | async-start | bytes 4718592 | tf_op jit(solution)/shard_map/all_to_all | solution.py:510
  40.2 0.0 copy-done
  40.2 0.0 copy-done.2
  40.2 0.0 copy-start.5
  40.2 0.9 copy-done.5
  41.2 0.0 copy-start.6
  41.2 0.9 copy-done.6
  42.1 0.0 copy-start.4
  42.1 8.2 %weights.1 = (bf16[32,64,256]{2,1,0:T(8,128)(2,1)S(1)}, bf16[64,4096]{1,0:T(8,128)(2,1)S(1)}) custom-call(s32[1]{0:T(128)} %bitcast.place_ref, f32[256,1024]{1,0:T(8,128)S(1)} %copy-done.2, f32[62,1024]{1,0:T(8,128)S(1)} %copy-done.5, f32[62,1024]{1,0:T(8,128)S(1)} %copy-done.6, f32[32,4096]{1,0:T(8,128)S(1)} %copy-done), custom_call_target="tpu_custom_call" | custom-call | flops 1000000000 | bytes 1048576 | tf_op jit(solution)/shard_map/weights/pallas_call | solution.py:524
  50.3 0.0 copy-start.1
  50.4 0.0 copy-done.4
  50.4 0.0 copy-done.7
  50.4 0.0 copy-done.8
  50.4 28.3 %near.1.near_hbm = f32[64,4096]{1,0:T(8,128)S(1)} custom-call(s32[32,27]{1,0:T(8,128)S(1)} %copy-done.7, f32[72,4096]{1,0:T(8,128)S(1)} %copy-done.8, f32[72,1024]{1,0:T(8,128)S(1)} %collective-permute-done.before_ref, f32[72,1024]{1,0:T(8,128)S(1)} %copy-done.4), custom_call_target="tpu_custom_call" | custom-call | flops 1000000000 | bytes 1048576 | tf_op jit(solution)/shard_map/near/pallas_call | solution.py:511
  78.6 17.5 %all-to-all-done.1.slots_ref = f32[32,144,128]{2,1,0:T(8,128)} async-done(((f32[32,144,128]{2,1,0:T(8,128)}), f32[32,144,128]{2,1,0:T(8,128)}, u32[]{:S(2)}, u32[]{:S(2)}) %all-to-all-start.1) | async-done | bytes 2359328 | tf_op jit(solution)/shard_map/all_to_all | solution.py:510
  96.2 0.0 copy-done.1
  96.2 5.1 %far.1 = f32[64,4096]{1,0:T(8,128)} custom-call(s32[1,256]{1,0:T(1,128)S(1)} %copy-done.1, f32[32,144,128]{2,1,0:T(8,128)} %all-to-all-done.1.slots_ref, bf16[32,64,256]{2,1,0:T(8,128)(2,1)S(1)} %get-tuple-element.20.coupling_hbm, f32[32,4096]{1,0:T(8,128)S(1)} %copy-done, bf16[64,4096]{1,0:T(8,128)(2,1)S(1)} %get-tuple-element.21.wide_basis_hbm, ...), custom_call_target="tpu_custom_call" | custom-call | flops 1000000000 | bytes 1048576 | tf_op jit(solution)/shard_map/far/pallas_call | solution.py:533
  (2 shorter events, 0.0 us)
Async XLA Ops:
  10.0 15.7 %collective-permute-start = (f32[72,1024]{1,0:T(8,128)}, f32[72,1024]{1,0:T(8,128)S(1)}, u32[]{:S(2)}, u32[]{:S(2)}) collective-permute-start(f32[72,1024]{1,0:T(8,128)} %get-tuple-element.16), channel_id=1, source_target_pairs={{0,1},{1,2},{2,3},{3,4},{4,5},{5,6},{6,7},{7,8},{8,9},{9,10},{10,1... | collective-permute-start | bytes 884744 | tf_op jit(solution)/shard_map/ppermute | solution.py:498
  12.9 12.8 %collective-permute-start.1 = (f32[72,1024]{1,0:T(8,128)}, f32[72,1024]{1,0:T(8,128)S(1)}, u32[]{:S(2)}, u32[]{:S(2)}) collective-permute-start(f32[72,1024]{1,0:T(8,128)} %get-tuple-element.17), channel_id=1, source_target_pairs={{1,0},{2,1},{3,2},{4,3},{5,4},{6,5},{7,6},{8,7},{9,8},{10,9},{11,1... | collective-permute-start | bytes 884744 | tf_op jit(solution)/shard_map/ppermute | solution.py:499
  15.3 10.4 %all-to-all-start = ((f32[8,16,128]{2,1,0:T(8,128)}), f32[8,16,128]{2,1,0:T(8,128)S(1)}, u32[]{:S(2)}, u32[]{:S(2)}) async-start(f32[8,16,128]{2,1,0:T(8,128)} %get-tuple-element.15), calls=%async_computation | async-start | bytes 131072 | tf_op jit(solution)/shard_map/all_to_all | solution.py:494
  25.7 0.6 copy-start.9
  26.3 2.0 %copy-start.3 = (f32[72,1024]{1,0:T(8,128)}, f32[72,1024]{1,0:T(8,128)S(1)}, u32[]{:S(2)}) copy-start(f32[72,1024]{1,0:T(8,128)S(1)} %collective-permute-done.1.after_ref) | copy-start | bytes 884740
  28.3 11.9 %copy-start = (f32[32,4096]{1,0:T(8,128)S(1)}, f32[32,4096]{1,0:T(8,128)}, u32[]{:S(2)}) copy-start(f32[32,4096]{1,0:T(8,128)} %basis_hbm.3) | copy-start | bytes 1572868
  28.3 11.9 %copy-start.2 = (f32[256,1024]{1,0:T(8,128)S(1)}, f32[256,1024]{1,0:T(8,128)}, u32[]{:S(2)}) copy-start(f32[256,1024]{1,0:T(8,128)} %coupling_in_ref.1) | copy-start | bytes 3145732
  28.3 67.9 %all-to-all-start.1 = ((f32[32,144,128]{2,1,0:T(8,128)}), f32[32,144,128]{2,1,0:T(8,128)}, u32[]{:S(2)}, u32[]{:S(2)}) async-start(f32[32,144,128]{2,1,0:T(8,128)} %top.1), calls=%async_computation.1 | async-start | bytes 4718592 | tf_op jit(solution)/shard_map/all_to_all | solution.py:510
  40.2 1.0 copy-start.5
  41.2 0.9 copy-start.6
  42.1 8.2 %copy-start.4 = (f32[72,1024]{1,0:T(8,128)S(1)}, f32[72,1024]{1,0:T(8,128)}, u32[]{:S(2)}) copy-start(f32[72,1024]{1,0:T(8,128)} %copy-done.3) | copy-start | bytes 884740
  42.1 8.2 %copy-start.7 = (s32[32,27]{1,0:T(8,128)S(1)}, s32[32,27]{1,0:T(8,128)}, u32[]{:S(2)}) copy-start(s32[32,27]{1,0:T(8,128)} %list_ref.1) | copy-start | bytes 10372
  42.1 8.2 %copy-start.8 = (f32[72,4096]{1,0:T(8,128)S(1)}, f32[72,4096]{1,0:T(8,128)}, u32[]{:S(2)}) copy-start(f32[72,4096]{1,0:T(8,128)} %get-tuple-element.22.points_ref) | copy-start | bytes 3538948
  50.3 45.8 %copy-start.1 = (s32[1,256]{1,0:T(1,128)S(1)}, s32[1,256]{1,0:T(1,128)}, u32[]{:S(2)}) copy-start(s32[1,256]{1,0:T(1,128)} %recv_ref.1) | copy-start | bytes 3076
